TPU v7x, 128 devices: a whole 4x4x4 slice. The times are simulated.
128 devices in a mesh: row: 16 (over z, y_hi, core), col: 8 (over y_lo, x).
Axes of the slice: x: 4, y: 4 (y_hi: 2, y_lo: 2; y = y_hi * 2 + y_lo), z: 4, core: 2. Of those that a mesh axis runs over, the one named last changes fastest.
Arguments:
- grad_hidden: bfloat16 [1024, 49152], P('row', 'col'), may hold values from -6 to 6
- pre_act: bfloat16 [1024, 49152], P('row', 'col'), may hold values from -6 to 6
- inputs: bfloat16 [1024, 12288], P('col', 'row'), may hold values from -6 to 6
- weight: bfloat16 [12288, 49152], P('row', 'col'), may hold values from -0.0546875 to 0.0546875
Outputs:
- grad_input: bfloat16 [1024, 12288], P('col', 'row')
- grad_weight: bfloat16 [12288, 49152], P('row', 'col')
All inputs are finite; a program needn't handle non-finite values.
Results may differ from a plain program's by a relative error of at most 0.017.
Values may be sent and summed in bfloat16 or wider, within the bound.
A program may use at most 128 MiB of HBM per device.

v0:
```python
import math

import jax
import jax.numpy as jnp
from jax import lax
from jax.sharding import PartitionSpec as P


def gelu_grad(value):
    coeff = math.sqrt(2.0 / math.pi)
    inner = coeff * (value + 0.044715 * value * value * value)
    tanh_value = jnp.tanh(inner)
    return 0.5 * (1.0 + tanh_value) + 0.5 * value * (1.0 - tanh_value * tanh_value) * coeff * (
        1.0 + 3.0 * 0.044715 * value * value
    )


def body(grad_hidden, pre_act, inputs, weight):
    grad_pre = (grad_hidden.astype(jnp.float32) * gelu_grad(pre_act.astype(jnp.float32))).astype(
        jnp.bfloat16
    )
    input_all = lax.all_gather(inputs, "col", axis=0, tiled=True)
    panel_all = lax.all_gather(grad_pre, "row", axis=0, tiled=True)
    partial_value = lax.dot_general(
        panel_all, weight, (((1,), (1,)), ((), ())), preferred_element_type=jnp.float32
    )
    weight_sum = lax.dot_general(
        input_all, panel_all, (((0,), (0,)), ((), ())), preferred_element_type=jnp.float32
    )
    grad_weight = weight_sum.astype(jnp.bfloat16)
    rounded = partial_value.astype(jnp.bfloat16)
    grad_input = (
        lax.psum_scatter(rounded, "col", scatter_dimension=0, tiled=True)
        .astype(jnp.float32)
        .astype(jnp.bfloat16)
    )
    return (grad_input, grad_weight)


def solution(mesh):
    return jax.shard_map(
        body,
        mesh=mesh,
        in_specs=(P("row", "col"), P("row", "col"), P("col", "row"), P("row", "col")),
        out_specs=(P("col", "row"), P("row", "col")),
        check_vma=False,
    )
```

profile of v0, /device:TPU:8, one launch (start us, length us, event | category | flops | bytes accessed | tf_op | source)
XLA Modules:
  0.0 192.8 jit_solution(7830295446037495804)
XLA Ops:
  7.2 0.0 all-gather.3.cloned.1.call-start
  7.2 3.3 %fusion.8 = bf16[64,6144]{1,0:T(8,128)(2,1)} fusion(bf16[64,6144]{1,0:T(8,128)(2,1)} %param.5, bf16[64,6144]{1,0:T(8,128)(2,1)} %param.4), kind=kLoop, calls=%fused_computation.17 | loop fusion | flops 8257536 | bytes 2359296 | tf_op jit(solution)/shard_map/convert_element_type | solution.py:19
  10.6 0.0 all-gather.3.cloned.1.call-update
  10.6 0.0 all-gather.5.cloned.1.call-start
  10.6 0.7 all-gather.5.cloned.1.call-update
  11.3 0.0 reduce-scatter.2.cloned.1.call-start
  11.4 92.0 %all-gather.3.cloned.1.call-done = bf16[1024,6144]{1,0:T(8,128)(2,1)} async-done(((bf16[64,6144]{1,0:T(8,128)(2,1)}), bf16[1024,6144]{1,0:T(8,128)(2,1)}) %all-gather.3.cloned.1.call-update) | async-done | bytes 12582928 | tf_op jit(solution)/shard_map/all_gather | solution.py:23
  103.4 15.7 %convolution_convert_fusion.1 = bf16[1024,768]{1,0:T(8,128)(2,1)} fusion(bf16[1024,6144]{1,0:T(8,128)(2,1)} %all-gather.3.cloned.1.call-done, bf16[768,6144]{1,0:T(8,128)(2,1)} %param.7), kind=kOutput, calls=%fused_computation.9 | convolution fusion | flops 9664462848 | bytes 23592960 | tf_op jit(solution)/shard_map/dot_general | solution.py:24
  119.1 0.0 reduce-scatter.2.cloned.1.call-update
  119.1 24.0 %all-gather.5.cloned.1.call-done = bf16[1024,768]{1,0:T(8,128)(2,1)} async-done(((bf16[128,768]{1,0:T(8,128)(2,1)}), bf16[1024,768]{1,0:T(8,128)(2,1)}) %all-gather.5.cloned.1.call-update) | async-done | bytes 1572880 | tf_op jit(solution)/shard_map/all_gather | solution.py:22
  143.1 15.7 %fusion = bf16[768,6144]{0,1:T(8,128)(2,1)} fusion(bf16[1024,6144]{1,0:T(8,128)(2,1)} %all-gather.3.cloned.1.call-done, bf16[1024,768]{1,0:T(8,128)(2,1)} %all-gather.5.cloned.1.call-done), kind=kOutput, calls=%fused_computation.1 | convolution fusion | flops 9668395008 | bytes 23592960 | tf_op jit(solution)/shard_map/dot_general | solution.py:27
  158.8 12.6 %copy.6 = bf16[768,6144]{1,0:T(8,128)(2,1)} copy(bf16[768,6144]{0,1:T(8,128)(2,1)} %fusion) | data formatting | bytes 18874368
  171.4 14.8 %reduce-scatter.2.cloned.1.call-done = bf16[128,768]{1,0:T(8,128)(2,1)} async-done(((bf16[1024,768]{1,0:T(8,128)(2,1)}), bf16[128,768]{1,0:T(8,128)(2,1)}) %reduce-scatter.2.cloned.1.call-update) | async-done | bytes 196624 | tf_op jit(solution)/shard_map/reduce_scatter | solution.py:33
Async XLA Ops:
  7.2 96.2 %all-gather.3.cloned.1.call-start = ((), (), s32[]{:S(2)}) async-start(), calls=%async_computation.1 | async-start | bytes 13369344 | tf_op jit(solution)/shard_map/all_gather | solution.py:23
  10.6 132.5 %all-gather.5.cloned.1.call-start = ((), (), s32[]{:S(2)}) async-start(), calls=%async_computation.3 | async-start | bytes 1769472 | tf_op jit(solution)/shard_map/all_gather | solution.py:22
  11.3 174.9 %reduce-scatter.2.cloned.1.call-start = ((), (), s32[]{:S(2)}) async-start(), calls=%async_computation.2 | async-start | bytes 1769472 | tf_op jit(solution)/shard_map/reduce_scatter | solution.py:33
Sparse Core Ops, SparseCore 0:
  11.0 92.2 all-gather.2
  105.0 38.0 all-gather.4
  146.1 40.1 reduce-scatter.1
where the time goes:
time: 194 us; the launch traced here: 193 us
  waiting for transfers between devices  132 us (68%)
  matrix products  31.4 us (16%)
  between operations  13.7 us (7%)
  local copies, waits for them, and re-layouts  12.6 us (6%)
  other arithmetic  3.34 us (2%)
    all_gather x1, waiting for transfers between devices, body(): panel_all = lax.all_gather(grad_pre, 'row', axis=0, tiled=True)  92 us
    all_gather x1, waiting for transfers between devices, body(): input_all = lax.all_gather(inputs, 'col', axis=0, tiled=True)  24 us
    dot_general x1, matrix products, body(): lax.dot_general(input_all, panel_all, (((0,), (0,)), ((), ())), preferred...  15.7 us
    dot_general x1, matrix products, body(): lax.dot_general(panel_all, weight, (((1,), (1,)), ((), ())), preferred_el...  15.7 us
    reduce_scatter x1, waiting for transfers between devices, body(): lax.psum_scatter(rounded, 'col', scatter_dimension=0, tiled=True)  14.8 us
    unnamed x1, local copies, waits for them, and re-layouts  12.6 us
  transfers between devices with their start and end apart: 3, of which 3 were waited for; matrix products, arithmetic and copies ran while one was open for 23% of the time, Pallas kernels for 0%

commit v1 on v0

v1 whole, which is shorter than its diff:
```python
import math

import jax
import jax.numpy as jnp
from jax import lax
from jax.experimental import pallas as pl
from jax.experimental.pallas import tpu as pltpu
from jax.sharding import PartitionSpec as P

NZ = 4
NX = 4
NCH = 6
NA = 4
GROUPS = ((0, 1), (2, 3), (4, 5))
NT = (((1,), (1,)), ((), ()))
NN = (((1,), (0,)), ((), ()))
BF16 = jnp.bfloat16
F32 = jnp.float32


def gelu_grad(value):
    coeff = math.sqrt(2.0 / math.pi)
    inner = coeff * (value + 0.044715 * value * value * value)
    tanh_value = jnp.tanh(inner)
    return 0.5 * (1.0 + tanh_value) + 0.5 * value * (1.0 - tanh_value * tanh_value) * coeff * (
        1.0 + 3.0 * 0.044715 * value * value
    )


def main_kernel(
    g_hbm, v_hbm, x_hbm, w_hbm,
    gi_ref, dw_ref,
    gbuf, vbuf, panel, wbuf, xbuf, xt, acc, sbuf, rx, ysend, yrecv,
    load_sem, w_sem, x_own_sem, send_sem, recv_sem, x_send, x_recv, rs_send, rs_recv, y_sem,
):
    r = lax.axis_index("row")
    c = lax.axis_index("col")
    z, yh, k = r // 4, (r // 2) % 2, r % 2
    yl, x = c // NX, c % NX
    tb = g_hbm.shape[0]
    cw = panel.shape[3]
    ob = x_hbm.shape[0]
    plane_rows = panel.shape[2]

    def at_row(dz, dy, dk):
        return lax.rem(z + dz, NZ) * 4 + lax.rem(yh + dy, 2) * 2 + lax.rem(k + dk, 2)

    def at_col(dyl, dx):
        return lax.rem(yl + dyl, 2) * NX + lax.rem(x + dx, NX)

    z_up, z_dn = (at_row(1, 0, 0), c), (at_row(3, 0, 0), c)
    y_other, core_other = (at_row(0, 1, 0), c), (at_row(0, 0, 1), c)

    loads = []
    for i in range(NCH):
        cols = pl.ds(i * cw, cw)
        pair = (
            pltpu.make_async_copy(g_hbm.at[:, cols], gbuf.at[i], load_sem.at[0, i]),
            pltpu.make_async_copy(v_hbm.at[:, cols], vbuf.at[i], load_sem.at[1, i]),
        )
        for cp in pair:
            cp.start()
        loads.append(pair)
    x_own = pltpu.make_async_copy(x_hbm, xbuf.at[c], x_own_sem)
    x_own.start()
    w_loads = []
    for i in range(NCH):
        cols = pl.ds(i * cw, cw)
        cp = pltpu.make_async_copy(w_hbm.at[:, cols], wbuf.at[:, cols], w_sem.at[i])
        cp.start()
        w_loads.append(cp)

    barrier = pltpu.get_barrier_semaphore()
    partners = [z_up, z_dn, y_other, core_other, (r, at_col(1, 0))]
    partners += [(r, at_col(0, dx)) for dx in (1, 2, 3)]
    for partner in partners:
        pl.semaphore_signal(barrier, inc=1, device_id=partner, device_id_type=pl.DeviceIdType.MESH)
    pl.semaphore_wait(barrier, len(partners))

    sends = []

    def remote(src, dst, s_sem, r_sem, target):
        return pltpu.make_async_remote_copy(
            src_ref=src, dst_ref=dst, send_sem=s_sem, recv_sem=r_sem,
            device_id=target, device_id_type=pl.DeviceIdType.MESH,
        )

    def block(dz, dy, dk, i):
        rows = lax.rem(yh + dy, 2) * (2 * tb) + lax.rem(k + dk, 2) * tb
        return panel.at[i, lax.rem(z + dz, NZ), pl.ds(pl.multiple_of(rows, tb), tb), :]

    def push(dz, dy, i, target, rz, ry, rk):
        here = block(dz, dy, 0, i)
        cp = remote(here, here, send_sem.at[len(sends)], recv_sem.at[rk, ry, rz, i], target)
        cp.start()
        sends.append(cp)

    def got(dz, dy, dk, i):
        here = block(dz, dy, dk, i)
        remote(here, here, send_sem.at[0], recv_sem.at[dk, dy, dz, i], core_other).wait_recv()

    def share(dz, dy, i):
        push(dz, dy, i, core_other, dz, dy, 1)

    def relay(dz, dy, i):
        if dz == 3 and i % 2 == 0:
            push(3, dy, i, z_up, 2, dy, 0)
        if dz == 1 and i % 2 == 1:
            push(1, dy, i, z_dn, 2, dy, 0)

    x_sends = []

    def send_x(cb, target, n, rs):
        cp = remote(xbuf.at[cb], xbuf.at[cb], x_send.at[n], rs, target)
        cp.start()
        x_sends.append(cp)

    def x_got(dyl, dx):
        here = xbuf.at[at_col(dyl, dx)]
        remote(here, here, x_send.at[0], x_recv.at[dyl, dx], core_other).wait_recv()

    for n, i in enumerate((4, 0, 5, 1, 2, 3)):
        for cp in loads[i]:
            cp.wait()
        value = gbuf[i].astype(F32) * gelu_grad(vbuf[i].astype(F32))
        panel[i, z, pl.ds(pl.multiple_of(yh * (2 * tb) + k * tb, tb), tb), :] = value.astype(BF16)
        push(0, 0, i, z_up, 3, 0, 0)
        push(0, 0, i, z_dn, 1, 0, 0)
        if i < NA:
            push(0, 0, i, y_other, 0, 1, 0)
        share(0, 0, i)
    for i in (4, 5):
        push(0, 0, i, y_other, 0, 1, 0)

    x_own.wait()
    send_x(c, (r, at_col(1, 0)), 0, x_recv.at[1, 0])
    for dx in (1, 2, 3):
        send_x(c, (r, at_col(0, dx)), dx, x_recv.at[0, NX - dx])

    def mm1(dz, group, first):
        plane = lax.rem(z + dz, NZ)
        term = None
        for i in GROUPS[group]:
            d = lax.dot_general(
                panel[i, plane], wbuf[:, i * cw:(i + 1) * cw], NT, preferred_element_type=F32
            )
            term = d if term is None else term + d
        acc[plane] = term if first else acc[plane] + term

    def mm2(dz, group, first):
        plane = lax.rem(z + dz, NZ)
        for i in GROUPS[group]:
            cols = slice(i * cw, (i + 1) * cw)
            d = lax.dot_general(xt[plane], panel[i, plane], NN, preferred_element_type=F32)
            dw_ref[:, cols] = d if first else dw_ref[:, cols] + d

    def transpose_x(dz):
        plane = lax.rem(z + dz, NZ)
        for h in range(2):
            xt[plane, :, h * ob:(h + 1) * ob] = xbuf[2 * plane + h].T

    def sib(dz, group, dys=(0, 1)):
        for dy in dys:
            for i in GROUPS[group]:
                got(dz, dy, 1, i)

    def rs_copy(dz, h):
        plane = lax.rem(z + dz, NZ)
        owner_yl = plane // 2
        target_x = 2 * lax.rem(plane, 2) + h
        slot = lax.rem(x - target_x + NX, NX)
        cp = remote(
            sbuf.at[2 * plane + h], rx.at[owner_yl, slot], rs_send.at[dz, h],
            rs_recv.at[owner_yl, slot], (r, yl * NX + target_x),
        )
        return cp, x != target_x

    def rs_start(dz):
        plane = lax.rem(z + dz, NZ)
        for h in range(2):
            sbuf[2 * plane + h] = acc[plane, h * ob:(h + 1) * ob, :].astype(BF16)
            cp, use = rs_copy(dz, h)
            pl.when(use)(cp.start)

    def rs_collect(owner_yl):
        plane = 2 * owner_yl + x // 2
        total = acc[plane, pl.ds(pl.multiple_of(lax.rem(x, 2) * ob, ob), ob), :]
        for slot in (1, 2, 3):
            here = rx.at[owner_yl, slot]
            remote(here, here, rs_send.at[0, 0], rs_recv.at[owner_yl, slot], core_other).wait_recv()
            total = total + rx[owner_yl, slot].astype(F32)
        return total

    for i in range(2):
        for dz in (3, 1):
            got(dz, 0, 0, 4 + i)
            push(dz, 0, 4 + i, y_other, dz, 1, 0)
            relay(dz, 0, 4 + i)
            share(dz, 0, 4 + i)
        got(0, 1, 0, i)
        push(0, 1, i, z_up, 3, 1, 0)
        push(0, 1, i, z_dn, 1, 1, 0)
        share(0, 1, i)
    x_got(1, 0)
    for dx in (1, 2, 3):
        send_x(at_col(1, 0), (r, at_col(0, dx)), 3 + dx, x_recv.at[1, NX - dx])
    for cp in w_loads:
        cp.wait()
    sib(0, 0)
    mm1(0, 0, True)
    for i in (2, 3):
        for dz in (3, 1):
            got(dz, 0, 0, i - 2)
            relay(dz, 0, i - 2)
            share(dz, 0, i - 2)
        got(0, 1, 0, i)
        push(0, 1, i, z_up, 3, 1, 0)
        push(0, 1, i, z_dn, 1, 1, 0)
        share(0, 1, i)
    sib(0, 1)
    mm1(0, 1, False)
    for i in (2, 3):
        for dz in (3, 1):
            got(dz, 0, 0, i)
            relay(dz, 0, i)
            share(dz, 0, i)
        got(0, 1, 0, 2 + i)
        share(0, 1, 2 + i)
    for dyl in range(2):
        for dx in (1, 2, 3):
            x_got(dyl, dx)
    for dz in range(NZ):
        transpose_x(dz)
    sib(0, 2)
    mm1(0, 2, False)
    rs_start(0)
    mm2(0, 0, True)
    got(2, 0, 0, 4)
    push(2, 0, 4, y_other, 2, 1, 0)
    share(2, 0, 4)
    for dz in (3, 1):
        got(dz, 1, 0, 0)
        relay(dz, 1, 0)
        share(dz, 1, 0)
    mm2(0, 1, True)
    got(2, 0, 0, 5)
    push(2, 0, 5, y_other, 2, 1, 0)
    share(2, 0, 5)
    mm2(0, 2, True)
    for dz in (3, 1):
        got(dz, 1, 0, 4)
        share(dz, 1, 4)
        got(dz, 1, 0, 1)
        relay(dz, 1, 1)
        share(dz, 1, 1)
    for dz in (3, 1):
        sib(dz, 0)
        mm1(dz, 0, True)
        mm2(dz, 0, False)
    for dz in (3, 1):
        got(dz, 1, 0, 2)
        relay(dz, 1, 2)
        share(dz, 1, 2)
        got(dz, 1, 0, 5)
        share(dz, 1, 5)
    for dz in (3, 1):
        sib(dz, 2)
        mm1(dz, 2, False)
        if dz == 3:
            for e in (3, 1):
                got(e, 1, 0, 3)
                relay(e, 1, 3)
                share(e, 1, 3)
        mm2(dz, 2, False)
    for i in range(NA):
        got(2, 0, 0, i)
        share(2, 0, i)
    for dz in (3, 1):
        sib(dz, 1)
        mm1(dz, 1, False)
        rs_start(dz)
    for i in (4, 5):
        got(2, 1, 0, i)
        share(2, 1, i)
    mm2(3, 1, False)
    sib(2, 2)
    mm1(2, 2, True)
    for i in (0, 1):
        got(2, 1, 0, i)
        share(2, 1, i)
    mm2(1, 1, False)
    sib(2, 0)
    mm1(2, 0, False)
    for i in (2, 3):
        got(2, 1, 0, i)
        share(2, 1, i)
    sib(2, 1)
    mm1(2, 1, False)
    rs_start(2)
    mm2(2, 0, False)
    mm2(2, 1, False)
    far = 1 - yl
    ysend[...] = rs_collect(far).astype(BF16)
    y_cp = remote(ysend, yrecv, y_sem.at[0], y_sem.at[1], (r, at_col(1, 0)))
    y_cp.start()
    mm2(2, 2, False)
    total = rs_collect(yl)
    y_cp.wait()
    gi_ref[...] = (total + yrecv[...].astype(F32)).astype(gi_ref.dtype)

    for cp in sends:
        cp.wait_send()
    for cp in x_sends:
        cp.wait_send()
    for dz in range(NZ):
        for h in range(2):
            cp, use = rs_copy(dz, h)
            pl.when(use)(cp.wait_send)


N_SENDS = 24 + 6 + 12 + 48
OUT_PARTS = 8


def out_kernel(gi_ref, dw_ref, gi_out, dw_out, buf, sem):
    part = dw_ref.shape[1] // OUT_PARTS
    gi_copy = pltpu.make_async_copy(gi_ref, gi_out, sem.at[OUT_PARTS])
    gi_copy.start()
    copies = []
    for i in range(OUT_PARTS):
        cols = pl.ds(i * part, part)
        buf[:, i * part:(i + 1) * part] = dw_ref[:, i * part:(i + 1) * part].astype(buf.dtype)
        cp = pltpu.make_async_copy(buf.at[:, cols], dw_out.at[:, cols], sem.at[i])
        cp.start()
        copies.append(cp)
    for cp in copies:
        cp.wait()
    gi_copy.wait()


def body(grad_hidden, pre_act, inputs, weight):
    tb, ft = grad_hidden.shape
    ob, dt = inputs.shape
    cw = ft // NCH
    tokens = 16 * tb
    hbm = pl.BlockSpec(memory_space=pltpu.HBM)
    vmem = pl.BlockSpec(memory_space=pltpu.VMEM)
    dma = pltpu.SemaphoreType.DMA
    gi, dw = pl.pallas_call(
        main_kernel,
        out_shape=(pltpu.VMEM((ob, dt), BF16), pltpu.VMEM((dt, ft), F32)),
        in_specs=[hbm] * 4,
        out_specs=(vmem, vmem),
        scratch_shapes=[
            pltpu.VMEM((NCH, tb, cw), BF16),
            pltpu.VMEM((NCH, tb, cw), BF16),
            pltpu.VMEM((NCH, NZ, tokens // NZ, cw), BF16),
            pltpu.VMEM((dt, ft), BF16),
            pltpu.VMEM((8, ob, dt), BF16),
            pltpu.VMEM((NZ, dt, tokens // NZ), BF16),
            pltpu.VMEM((NZ, tokens // NZ, dt), F32),
            pltpu.VMEM((8, ob, dt), BF16),
            pltpu.VMEM((2, NX, ob, dt), BF16),
            pltpu.VMEM((ob, dt), BF16),
            pltpu.VMEM((ob, dt), BF16),
            dma((2, NCH)),
            dma((NCH,)),
            dma,
            dma((N_SENDS,)),
            dma((2, 2, NZ, NCH)),
            dma((7,)),
            dma((2, NX)),
            dma((NZ, 2)),
            dma((2, NX)),
            dma((2,)),
        ],
        compiler_params=pltpu.CompilerParams(
            collective_id=0, has_side_effects=True, vmem_limit_bytes=44 * 2**20
        ),
        name="gather_and_multiply",
    )(grad_hidden, pre_act, inputs, weight)
    return pl.pallas_call(
        out_kernel,
        out_shape=(
            jax.ShapeDtypeStruct((ob, dt), BF16),
            jax.ShapeDtypeStruct((dt, ft), BF16),
        ),
        in_specs=[vmem, vmem],
        out_specs=(hbm, hbm),
        scratch_shapes=[pltpu.VMEM((dt, ft), BF16), dma((OUT_PARTS + 1,))],
        compiler_params=pltpu.CompilerParams(vmem_limit_bytes=20 * 2**20),
        name="round_and_write",
    )(gi, dw)


def solution(mesh):
    return jax.shard_map(
        body,
        mesh=mesh,
        in_specs=(P("row", "col"), P("row", "col"), P("col", "row"), P("row", "col")),
        out_specs=(P("col", "row"), P("row", "col")),
        check_vma=False,
    )
```

time: 194 us -> 88.6 us (0.46)
  waiting for transfers between devices: 132 us -> 0 us
  Pallas kernels: 0 us -> 87.7 us
  matrix products: 31.4 us -> 0 us
  between operations: 13.7 us -> 0.82 us
  local copies, waits for them, and re-layouts: 12.6 us -> 0 us
  other arithmetic: 3.34 us -> 0 us
    all_gather x2 -> x0, waiting for transfers between devices: 116 us -> none  [the longest x1 92 us: body(): panel_all = lax.all_gather(grad_pre, 'row', axis=0, tiled=True)]
    pallas_call x0 -> x2, Pallas kernels: none -> 87.7 us  [the longest x1 83.9 us: body(): pl.pallas_call(main_kernel, out_shape=(pltpu.VMEM((ob, dt), BF16), pltpu....]
    dot_general x2 -> x0, matrix products: 31.4 us -> none  [the longest x1 15.7 us: body(): lax.dot_general(input_all, panel_all, (((0,), (0,)), ((), ())), preferred...]
    reduce_scatter x1 -> x0, waiting for transfers between devices: 14.8 us -> none  [body(): lax.psum_scatter(rounded, 'col', scatter_dimension=0, tiled=True)]
    unnamed x1 -> x0, local copies, waits for them, and re-layouts: 12.6 us -> none
    convert_element_type x1 -> x0, other arithmetic: 3.34 us -> none  [body(): (grad_hidden.astype(jnp.float32) * gelu_grad(pre_act.astype(jnp.float32))...]
  transfers between devices with their start and end apart: 3 -> 0, of which waited for: 3 -> 0; matrix products, arithmetic and copies ran while one was open for 23% -> 0% of each run, Pallas kernels for 0% -> 0%
where the time goes in v1:
time: 88.6 us; the launch traced here: 88.5 us
  Pallas kernels  87.7 us (99%)
    pallas_call x1, Pallas kernels, body(): pl.pallas_call(main_kernel, out_shape=(pltpu.VMEM((ob, dt), BF16), pltpu....  83.9 us
    pallas_call x1, Pallas kernels, body(): pl.pallas_call(out_kernel, out_shape=(jax.ShapeDtypeStruct((ob, dt), BF16...  3.83 us

profile of v1, /device:TPU:8, one launch (start us, length us, event | category | flops | bytes accessed | tf_op | source)
XLA Modules:
  0.0 88.5 jit_solution(11908829676179877754)
XLA Ops:
  0.6 83.9 %gather_and_multiply.1 = (bf16[128,768]{1,0:T(8,128)(2,1)S(1)}, f32[768,6144]{1,0:T(8,128)S(1)}) custom-call(bf16[64,6144]{1,0:T(8,128)(2,1)} %g_hbm.1, bf16[64,6144]{1,0:T(8,128)(2,1)} %v_hbm.1, bf16[128,768]{1,0:T(8,128)(2,1)} %x_hbm.1, bf16[768,6144]{1,0:T(8,128)(2,1)} %w_hbm.1), custom_call_target="tpu_custom_call" | custom-call | tf_op jit(solution)/shard_map/gather_and_multiply/pallas_call | solution.py:349
  84.5 3.8 %round_and_write.1 = (bf16[128,768]{1,0:T(8,128)(2,1)}, bf16[768,6144]{1,0:T(8,128)(2,1)}) custom-call(bf16[128,768]{1,0:T(8,128)(2,1)S(1)} %get-tuple-element.4.gi_ref, f32[768,6144]{1,0:T(8,128)S(1)} %get-tuple-element.5.dw_ref), custom_call_target="tpu_custom_call" | custom-call | tf_op jit(solution)/shard_map/round_and_write/pallas_call | solution.py:382

commit v2 on v0

v2 whole, which is shorter than its diff:
```python
import math

import jax
import jax.numpy as jnp
from jax import lax
from jax.experimental import pallas as pl
from jax.experimental.pallas import tpu as pltpu
from jax.sharding import PartitionSpec as P

NZ = 4
NX = 4
NCH = 6
NA = 4
GROUPS = ((0, 1), (2, 3), (4, 5))
MM1 = (
    (0, 0), (0, 1), (3, 0), (1, 0), (3, 1), (1, 1), (3, 2), (1, 2), (0, 2), None, None, (2, 2), (2, 0), (2, 1),
    None, None,
)
MM2 = (
    None, (0, 0), (0, 1), (3, 0), (1, 0), None, None, (3, 1), (1, 1), (3, 2), (1, 2), (0, 2), None, (2, 2),
    (2, 0), (2, 1),
)
STEPS = len(MM1)
NT = (((1,), (1,)), ((), ()))
NN = (((1,), (0,)), ((), ()))
BF16 = jnp.bfloat16
F32 = jnp.float32


def gelu_grad(value):
    coeff = math.sqrt(2.0 / math.pi)
    inner = coeff * (value + 0.044715 * value * value * value)
    tanh_value = jnp.tanh(inner)
    return 0.5 * (1.0 + tanh_value) + 0.5 * value * (1.0 - tanh_value * tanh_value) * coeff * (
        1.0 + 3.0 * 0.044715 * value * value
    )


def main_kernel(
    g_hbm, v_hbm, x_hbm, w_hbm,
    gi_ref, dw_ref,
    gbuf, vbuf, panel, wbuf, xbuf, xt, acc, sbuf, rx, stage, parts,
    load_sem, w_sem, x_own_sem, send_sem, recv_sem, x_send, x_recv, rs_send, rs_recv, own_send, own_recv,
):
    r = lax.axis_index("row")
    c = lax.axis_index("col")
    z, yh, k = r // 4, (r // 2) % 2, r % 2
    yl, x = c // NX, c % NX
    tb = g_hbm.shape[0]
    cw = panel.shape[3]
    ob = x_hbm.shape[0]
    plane_rows = panel.shape[2]

    def at_row(dz, dy, dk):
        return lax.rem(z + dz, NZ) * 4 + lax.rem(yh + dy, 2) * 2 + lax.rem(k + dk, 2)

    def at_col(dyl, dx):
        return lax.rem(yl + dyl, 2) * NX + lax.rem(x + dx, NX)

    z_up, z_dn = (at_row(1, 0, 0), c), (at_row(3, 0, 0), c)
    y_other, core_other = (at_row(0, 1, 0), c), (at_row(0, 0, 1), c)

    x_own = pltpu.make_async_copy(x_hbm, xbuf.at[c], x_own_sem)
    x_own.start()
    loads = []
    for i in range(NCH):
        cols = pl.ds(i * cw, cw)
        pair = (
            pltpu.make_async_copy(g_hbm.at[:, cols], gbuf.at[i], load_sem.at[0, i]),
            pltpu.make_async_copy(v_hbm.at[:, cols], vbuf.at[i], load_sem.at[1, i]),
        )
        for cp in pair:
            cp.start()
        loads.append(pair)
    barrier = pltpu.get_barrier_semaphore()
    partners = [z_up, z_dn, y_other, core_other, (r, at_col(1, 0))]
    partners += [(r, at_col(0, dx)) for dx in (1, 2, 3)]
    for partner in partners:
        pl.semaphore_signal(barrier, inc=1, device_id=partner, device_id_type=pl.DeviceIdType.MESH)
    pl.semaphore_wait(barrier, len(partners))

    sends = []

    def remote(src, dst, s_sem, r_sem, target):
        return pltpu.make_async_remote_copy(
            src_ref=src, dst_ref=dst, send_sem=s_sem, recv_sem=r_sem,
            device_id=target, device_id_type=pl.DeviceIdType.MESH,
        )

    def block(dz, dy, dk, i):
        rows = lax.rem(yh + dy, 2) * (2 * tb) + lax.rem(k + dk, 2) * tb
        return panel.at[i, lax.rem(z + dz, NZ), pl.ds(pl.multiple_of(rows, tb), tb), :]

    def push(dz, dy, i, target, rz, ry, rk):
        here = block(dz, dy, 0, i)
        remote(here, here, send_sem.at[len(sends)], recv_sem.at[rk, ry, rz, i], target).start()
        sends.append(i)

    def got(dz, dy, dk, i):
        here = block(dz, dy, dk, i)
        remote(here, here, send_sem.at[0], recv_sem.at[dk, dy, dz, i], core_other).wait_recv()

    def share(dz, dy, i):
        push(dz, dy, i, core_other, dz, dy, 1)

    def relay(dz, dy, i):
        if dz == 3 and i % 2 == 0:
            push(3, dy, i, z_up, 2, dy, 0)
        if dz == 1 and i % 2 == 1:
            push(1, dy, i, z_dn, 2, dy, 0)

    def send_x(cb, target, n, rs):
        remote(xbuf.at[cb], xbuf.at[cb], x_send.at[n], rs, target).start()

    def x_got(dyl, dx):
        here = xbuf.at[at_col(dyl, dx)]
        remote(here, here, x_send.at[0], x_recv.at[dyl, dx], core_other).wait_recv()

    x_own.wait()
    send_x(c, (r, at_col(1, 0)), 0, x_recv.at[1, 0])
    for dx in (1, 2, 3):
        send_x(c, (r, at_col(0, dx)), dx, x_recv.at[0, NX - dx])

    for i in range(NCH):
        for cp in loads[i]:
            cp.wait()
        value = gbuf[i].astype(F32) * gelu_grad(vbuf[i].astype(F32))
        panel[i, z, pl.ds(pl.multiple_of(yh * (2 * tb) + k * tb, tb), tb), :] = value.astype(BF16)
        push(0, 0, i, z_up, 3, 0, 0)
        push(0, 0, i, z_dn, 1, 0, 0)
        if i < NA:
            push(0, 0, i, y_other, 0, 1, 0)
        share(0, 0, i)

    w_loads = []
    for i in range(NCH):
        cols = pl.ds(i * cw, cw)
        cp = pltpu.make_async_copy(w_hbm.at[:, cols], wbuf.at[i], w_sem.at[i])
        cp.start()
        w_loads.append(cp)

    def packed(values, step):
        word = sum(v << (2 * n) for n, v in enumerate(values))
        return lax.shift_right_arithmetic(jnp.int32(word - (1 << 32) if word >> 31 else word), 2 * step) & 3

    def unit(units, step):
        dz = packed([u[0] if u else 0 for u in units], step)
        return lax.rem(z + dz, NZ), packed([u[1] if u else 0 for u in units], step)

    def busy(units, step):
        return packed([0 if u is None else 1 for u in units], step) == 1

    def choose(step, what, lo, hi):
        if hi - lo == 1:
            what(lo)
        else:
            mid = (lo + hi) // 2
            lax.cond(
                step < mid, lambda: choose(step, what, lo, mid), lambda: choose(step, what, mid, hi)
            )

    def mm1(step):
        plane, group = unit(MM1, step)
        term = None
        for j in range(2):
            i = 2 * group + j
            d = lax.dot_general(panel[i, plane], wbuf[i], NT, preferred_element_type=F32)
            term = d if term is None else term + d
        acc[plane] = acc[plane] + term

    def mm2(step):
        plane, group = unit(MM2, step)
        for j in range(2):
            i = 2 * group + j
            d = lax.dot_general(xt[plane], panel[i, plane], NN, preferred_element_type=F32)
            dw_ref[i] = dw_ref[i] + d

    def transpose_x(dz):
        plane = lax.rem(z + dz, NZ)
        for h in range(2):
            xt[plane, :, h * ob:(h + 1) * ob] = xbuf[2 * plane + h].T

    def sib(dz, group, dys=(0, 1)):
        for dy in dys:
            for i in GROUPS[group]:
                got(dz, dy, 1, i)

    def quarter(plane, xc):
        near = xc // 2 == lax.rem(plane, 2)
        half = jnp.where(near, lax.rem(xc, 2), 1 - lax.rem(xc, 2))
        return pl.multiple_of(half * ob + jnp.where(near, 0, tb), tb)

    def rs_copy(dz, dx):
        plane = lax.rem(z + dz, NZ)
        rows = pl.ds(quarter(plane, lax.rem(x + dx, NX)), tb)
        return remote(
            sbuf.at[plane, rows, :], rx.at[dz, dx - 1], rs_send.at[dz, dx - 1], rs_recv.at[dz, dx - 1],
            (r, at_col(0, dx)),
        )

    def rs_start(dz):
        plane = lax.rem(z + dz, NZ)
        sbuf[plane] = acc[plane].astype(BF16)
        for dx in (1, 2, 3):
            rs_copy(dz, dx).start()

    def own_copy(dz):
        plane = lax.rem(z + dz, NZ)
        near = x // 2 == lax.rem(plane, 2)
        j = jnp.where(near, 0, 1)
        owner_x = jnp.where(near, x, 3 - x)
        owner_yl = plane // 2
        rel = lax.rem(owner_yl + yl, 2)
        cp = remote(
            stage.at[dz], parts.at[j, rel], own_send.at[dz], own_recv.at[j, rel], (r, owner_yl * NX + owner_x)
        )
        return cp, jnp.logical_or(owner_x != x, owner_yl != yl)

    def rs_collect(dz):
        plane = lax.rem(z + dz, NZ)
        total = acc[plane, pl.ds(quarter(plane, x), tb), :]
        for dx in (1, 2, 3):
            rs_copy(dz, dx).wait_recv()
            total = total + rx[dz, dx - 1].astype(F32)
        stage[dz] = total.astype(BF16)
        cp, away = own_copy(dz)
        pl.when(away)(cp.start)

    def rs_finish():
        mine = lax.rem(c // 2 - z + NZ, NZ)
        for j in range(2):
            for rel in range(2):
                if j or rel:
                    here = parts.at[j, rel]
                    remote(here, here, own_send.at[0], own_recv.at[j, rel], core_other).wait_recv()
            first = parts[1, 0] if j else stage[mine]
            total = first.astype(F32) + parts[j, 1].astype(F32)
            gi_ref[j * tb:(j + 1) * tb, :] = total.astype(gi_ref.dtype)

    def near(i):
        for dz in (3, 1):
            got(dz, 0, 0, i)
            if i >= NA:
                push(dz, 0, i, y_other, dz, 1, 0)
            share(dz, 0, i)

    def other(i):
        got(0, 1, 0, i)
        if i < NA:
            push(0, 1, i, z_up, 3, 1, 0)
            push(0, 1, i, z_dn, 1, 1, 0)
        share(0, 1, i)

    def near_other(i):
        for dz in (3, 1):
            got(dz, 1, 0, i)
            if i < NA:
                relay(dz, 1, i)
            share(dz, 1, i)

    def far(i):
        got(2, 0, 0, i)
        if i >= NA:
            push(2, 0, i, y_other, 2, 1, 0)
        share(2, 0, i)

    def far_other(i):
        got(2, 1, 0, i)
        share(2, 1, i)

    def forward_x():
        x_got(1, 0)
        for dx in (1, 2, 3):
            send_x(at_col(1, 0), (r, at_col(0, dx)), 3 + dx, x_recv.at[1, NX - dx])

    def clear(chunks):
        for i in chunks:
            dw_ref[i] = jnp.zeros_like(dw_ref[i])

    def before(n):
        if n == 0:
            acc[...] = jnp.zeros_like(acc)
            near(0)
            other(0)
            forward_x()
            clear((0, 1))
            near(1)
            other(1)
            clear((2, 3))
            for cp in w_loads:
                cp.wait()
        if n == 1:
            near(2)
            clear((4, 5))
            near(3)
            other(2)
            near(4)
            other(3)
            near(5)
            for i in (4, 5):
                push(0, 0, i, y_other, 0, 1, 0)
            for i in (4, 5, 0, 1, 2, 3):
                for dz in (3, 1):
                    relay(dz, 0, i)
        if n == 2:
            near_other(0)
            near_other(1)
        if n == 4:
            near_other(2)
            near_other(3)
        if n == 5:
            near_other(4)
            near_other(5)
        if n == 6:
            far(4)
            far(5)
        if n == 7:
            other(4)
            other(5)
        if n == 9:
            far(0)
            far(1)
        if n == 10:
            far(2)
            far(3)
        if n == 11:
            far_other(4)
            far_other(5)
            far_other(0)
            far_other(1)
        if n == 12:
            far_other(2)
            far_other(3)
        if MM1[n] is not None:
            sib(*MM1[n])
        if n == 14:
            rs_collect(0)

    def between(n):
        if n == 1:
            for dyl in range(2):
                for dx in (1, 2, 3):
                    x_got(dyl, dx)
            for dz in range(NZ):
                transpose_x(dz)
        for dz, last in ((3, 6), (1, 7), (0, 8), (2, 13)):
            if n == last:
                rs_start(dz)
        if n == 13:
            rs_collect(3)
            rs_collect(1)

    @pl.loop(0, STEPS)
    def _(step):
        choose(step, before, 0, STEPS)
        pl.when(busy(MM1, step))(lambda: mm1(step))
        choose(step, between, 0, STEPS)
        pl.when(busy(MM2, step))(lambda: mm2(step))

    rs_collect(2)
    rs_finish()

    for n in range(len(sends)):
        here = block(0, 0, 0, 0)
        remote(here, here, send_sem.at[n], recv_sem.at[0, 0, 0, 0], core_other).wait_send()
    for n in range(7):
        remote(xbuf.at[c], xbuf.at[c], x_send.at[n], x_recv.at[0, 0], core_other).wait_send()
    for dz in range(NZ):
        for dx in (1, 2, 3):
            rs_copy(dz, dx).wait_send()
        cp, away = own_copy(dz)
        pl.when(away)(cp.wait_send)


N_SENDS = 24 + 6 + 12 + 48


def out_kernel(gi_ref, dw_ref, gi_out, dw_out, buf, sem):
    cw = dw_ref.shape[2]
    gi_copy = pltpu.make_async_copy(gi_ref, gi_out, sem.at[NCH])
    gi_copy.start()
    copies = []
    for i in range(NCH):
        buf[i] = dw_ref[i].astype(buf.dtype)
        cp = pltpu.make_async_copy(buf.at[i], dw_out.at[:, pl.ds(i * cw, cw)], sem.at[i])
        cp.start()
        copies.append(cp)
    for cp in copies:
        cp.wait()
    gi_copy.wait()


def body(grad_hidden, pre_act, inputs, weight):
    tb, ft = grad_hidden.shape
    ob, dt = inputs.shape
    cw = ft // NCH
    tokens = 16 * tb
    hbm = pl.BlockSpec(memory_space=pltpu.HBM)
    vmem = pl.BlockSpec(memory_space=pltpu.VMEM)
    dma = pltpu.SemaphoreType.DMA
    gi, dw = pl.pallas_call(
        main_kernel,
        out_shape=(pltpu.VMEM((ob, dt), BF16), pltpu.VMEM((NCH, dt, cw), F32)),
        in_specs=[hbm] * 4,
        out_specs=(vmem, vmem),
        scratch_shapes=[
            pltpu.VMEM((NCH, tb, cw), BF16),
            pltpu.VMEM((NCH, tb, cw), BF16),
            pltpu.VMEM((NCH, NZ, tokens // NZ, cw), BF16),
            pltpu.VMEM((NCH, dt, cw), BF16),
            pltpu.VMEM((8, ob, dt), BF16),
            pltpu.VMEM((NZ, dt, tokens // NZ), BF16),
            pltpu.VMEM((NZ, tokens // NZ, dt), F32),
            pltpu.VMEM((NZ, tokens // NZ, dt), BF16),
            pltpu.VMEM((NZ, NX - 1, tb, dt), BF16),
            pltpu.VMEM((NZ, tb, dt), BF16),
            pltpu.VMEM((2, 2, tb, dt), BF16),
            dma((2, NCH)),
            dma((NCH,)),
            dma,
            dma((N_SENDS,)),
            dma((2, 2, NZ, NCH)),
            dma((7,)),
            dma((2, NX)),
            dma((NZ, NX - 1)),
            dma((NZ, NX - 1)),
            dma((NZ,)),
            dma((2, 2)),
        ],
        compiler_params=pltpu.CompilerParams(
            collective_id=0, has_side_effects=True, vmem_limit_bytes=44 * 2**20
        ),
        name="gather_and_multiply",
    )(grad_hidden, pre_act, inputs, weight)
    return pl.pallas_call(
        out_kernel,
        out_shape=(
            jax.ShapeDtypeStruct((ob, dt), BF16),
            jax.ShapeDtypeStruct((dt, ft), BF16),
        ),
        in_specs=[vmem, vmem],
        out_specs=(hbm, hbm),
        scratch_shapes=[pltpu.VMEM((NCH, dt, cw), BF16), dma((NCH + 1,))],
        compiler_params=pltpu.CompilerParams(vmem_limit_bytes=20 * 2**20),
        name="round_and_write",
    )(gi, dw)


def solution(mesh):
    return jax.shard_map(
        body,
        mesh=mesh,
        in_specs=(P("row", "col"), P("row", "col"), P("col", "row"), P("row", "col")),
        out_specs=(P("col", "row"), P("row", "col")),
        check_vma=False,
    )
```

time: 194 us -> 76.6 us (0.39)
  waiting for transfers between devices: 132 us -> 0 us
  Pallas kernels: 0 us -> 75.8 us
  matrix products: 31.4 us -> 0 us
  between operations: 13.7 us -> 0.64 us
  local copies, waits for them, and re-layouts: 12.6 us -> 0 us
  other arithmetic: 3.34 us -> 0 us
    all_gather x2 -> x0, waiting for transfers between devices: 116 us -> none  [the longest x1 92 us: body(): panel_all = lax.all_gather(grad_pre, 'row', axis=0, tiled=True)]
    pallas_call x0 -> x2, Pallas kernels: none -> 75.8 us  [the longest x1 72 us: body(): pl.pallas_call(main_kernel, out_shape=(pltpu.VMEM((ob, dt), BF16), pltpu....]
    dot_general x2 -> x0, matrix products: 31.4 us -> none  [the longest x1 15.7 us: body(): lax.dot_general(input_all, panel_all, (((0,), (0,)), ((), ())), preferred...]
    reduce_scatter x1 -> x0, waiting for transfers between devices: 14.8 us -> none  [body(): lax.psum_scatter(rounded, 'col', scatter_dimension=0, tiled=True)]
    unnamed x1 -> x0, local copies, waits for them, and re-layouts: 12.6 us -> none
    convert_element_type x1 -> x0, other arithmetic: 3.34 us -> none  [body(): (grad_hidden.astype(jnp.float32) * gelu_grad(pre_act.astype(jnp.float32))...]
  transfers between devices with their start and end apart: 3 -> 0, of which waited for: 3 -> 0; matrix products, arithmetic and copies ran while one was open for 23% -> 0% of each run, Pallas kernels for 0% -> 0%
where the time goes in v2:
time: 76.6 us; the launch traced here: 76.5 us
  Pallas kernels  75.8 us (99%)
    pallas_call x1, Pallas kernels, body(): pl.pallas_call(main_kernel, out_shape=(pltpu.VMEM((ob, dt), BF16), pltpu....  72 us
    pallas_call x1, Pallas kernels, body(): pl.pallas_call(out_kernel, out_shape=(jax.ShapeDtypeStruct((ob, dt), BF16...  3.86 us

profile of v2, /device:TPU:8, one launch (start us, length us, event | category | flops | bytes accessed | tf_op | source)
XLA Modules:
  0.0 76.5 jit_solution(16957322445900257222)
XLA Ops:
  0.6 72.0 %gather_and_multiply.1 = (bf16[128,768]{1,0:T(8,128)(2,1)S(1)}, f32[6,768,1024]{2,1,0:T(8,128)S(1)}) custom-call(bf16[64,6144]{1,0:T(8,128)(2,1)} %g_hbm.1, bf16[64,6144]{1,0:T(8,128)(2,1)} %v_hbm.1, bf16[128,768]{1,0:T(8,128)(2,1)} %x_hbm.1, bf16[768,6144]{1,0:T(8,128)(2,1)} %w_hbm.1), custom_call_target="tpu_custom_call" | custom-call | tf_op jit(solution)/shard_map/gather_and_multiply/pallas_call | solution.py:401
  72.6 3.9 %round_and_write.1 = (bf16[128,768]{1,0:T(8,128)(2,1)}, bf16[768,6144]{1,0:T(8,128)(2,1)}) custom-call(bf16[128,768]{1,0:T(8,128)(2,1)S(1)} %get-tuple-element.4.gi_ref, f32[6,768,1024]{2,1,0:T(8,128)S(1)} %get-tuple-element.5.dw_ref), custom_call_target="tpu_custom_call" | custom-call | tf_op jit(solution)/shard_map/round_and_write/pallas_call | solution.py:435

commit v3 on v2

v3 whole, which is shorter than its diff:
```python
import math

import jax
import jax.numpy as jnp
from jax import lax
from jax.experimental import pallas as pl
from jax.experimental.pallas import tpu as pltpu
from jax.sharding import PartitionSpec as P

NZ = 4
NX = 4
NCH = 6
NA = 4
GROUPS = ((0, 1), (2, 3), (4, 5))
OWN, NEAR, CROSS, FAR = range(4)
STEP = (
    ((NEAR, 0), None, None),
    ((OWN, 0), None, None),
    ((NEAR, 1), None, None),
    ((OWN, 1), None, None),
    ((NEAR, 2), None, (OWN, 0)),
    (None, None, (NEAR, 0)),
    (None, None, (OWN, 1)),
    ((CROSS, 0), None, (NEAR, 1)),
    (None, None, (NEAR, 2)),
    ((OWN, 2), None, (OWN, 2)),
    ((CROSS, 1), None, None),
    ((CROSS, 2), None, (CROSS, 0)),
    (None, (0, 0), None),
    (None, (0, 1), None),
    (None, (0, 2), (CROSS, 1)),
    (None, (1, 2), None),
    (None, (1, 0), None),
    (None, (1, 1), (CROSS, 2)),
    (None, None, (FAR, 2)),
    (None, None, (FAR, 0)),
    (None, None, (FAR, 1)),
)
MM1, MM1H, MM2 = zip(*STEP)
STEPS = len(STEP)
NT = (((1,), (1,)), ((), ()))
NN = (((1,), (0,)), ((), ()))
BF16 = jnp.bfloat16
F32 = jnp.float32


def gelu_grad(value):
    coeff = math.sqrt(2.0 / math.pi)
    inner = coeff * (value + 0.044715 * value * value * value)
    tanh_value = jnp.tanh(inner)
    return 0.5 * (1.0 + tanh_value) + 0.5 * value * (1.0 - tanh_value * tanh_value) * coeff * (
        1.0 + 3.0 * 0.044715 * value * value
    )


def main_kernel(
    g_hbm, v_hbm, x_hbm, w_hbm,
    gi_ref, dw_ref,
    gbuf, vbuf, panel, wbuf, xbuf, xt, acc, acc2, sbuf, rx, stage, parts,
    load_sem, w_sem, x_own_sem, send_sem, recv_sem, far_sem, x_send, x_recv, rs_send, rs_recv, rs2_send, rs2_recv,
    own_send, own2_send, own_recv,
):
    r = lax.axis_index("row")
    c = lax.axis_index("col")
    z, yh, k = r // 4, (r // 2) % 2, r % 2
    yl, x = c // NX, c % NX
    tb = g_hbm.shape[0]
    cw = panel.shape[3]
    ob = x_hbm.shape[0]

    def at_row(dz, dy, dk):
        return lax.rem(z + dz, NZ) * 4 + lax.rem(yh + dy, 2) * 2 + lax.rem(k + dk, 2)

    def at_col(dyl, dx):
        return lax.rem(yl + dyl, 2) * NX + lax.rem(x + dx, NX)

    z_up, z_dn = (at_row(1, 0, 0), c), (at_row(3, 0, 0), c)
    y_other, core_other = (at_row(0, 1, 0), c), (at_row(0, 0, 1), c)

    x_own = pltpu.make_async_copy(x_hbm, xbuf.at[c], x_own_sem)
    x_own.start()
    loads = []
    for i in range(NCH):
        cols = pl.ds(i * cw, cw)
        pair = (
            pltpu.make_async_copy(g_hbm.at[:, cols], gbuf.at[i], load_sem.at[0, i]),
            pltpu.make_async_copy(v_hbm.at[:, cols], vbuf.at[i], load_sem.at[1, i]),
        )
        for cp in pair:
            cp.start()
        loads.append(pair)
    barrier = pltpu.get_barrier_semaphore()
    partners = [z_up, z_dn, y_other, core_other, (r, at_col(1, 0))]
    partners += [(r, at_col(0, dx)) for dx in (1, 2, 3)]
    for partner in partners:
        pl.semaphore_signal(barrier, inc=1, device_id=partner, device_id_type=pl.DeviceIdType.MESH)
    pl.semaphore_wait(barrier, len(partners))

    hb = tb // 2
    n_sent = [0]
    n_sent2 = [0]

    def remote(src, dst, s_sem, r_sem, target):
        return pltpu.make_async_remote_copy(
            src_ref=src, dst_ref=dst, send_sem=s_sem, recv_sem=r_sem,
            device_id=target, device_id_type=pl.DeviceIdType.MESH,
        )

    def owned(dz, dy):
        return 2 * lax.rem(z + dz, NZ) + lax.rem(yh + dy, 2)

    def block(dz, dy, dk, i):
        rows = pl.ds(pl.multiple_of(lax.rem(k + dk, 2) * tb, tb), tb)
        return panel.at[i, owned(dz, dy), rows, :]

    def half(dz, dy, dk, i, p):
        rows = pl.ds(pl.multiple_of(lax.rem(k + dk, 2) * tb + p * hb, hb), hb)
        return panel.at[i, owned(dz, dy), rows, :]

    def push(dz, dy, i, target, rz, ry, rk):
        here = block(dz, dy, 0, i)
        remote(here, here, send_sem.at[n_sent[0]], recv_sem.at[rk, ry, rz, i], target).start()
        n_sent[0] += 1

    def push2(dz, dy, i, p, target, ry, rk):
        here = half(dz, dy, 0, i, p)
        remote(here, here, send_sem.at[N_SENDS + n_sent2[0]], far_sem.at[rk, ry, i, p], target).start()
        n_sent2[0] += 1

    def got(dz, dy, dk, i):
        here = block(dz, dy, dk, i)
        remote(here, here, send_sem.at[0], recv_sem.at[dk, dy, dz, i], core_other).wait_recv()

    def got2(dy, dk, i, p):
        here = half(2, dy, dk, i, p)
        remote(here, here, send_sem.at[0], far_sem.at[dk, dy, i, p], core_other).wait_recv()

    def share(dz, dy, i):
        push(dz, dy, i, core_other, dz, dy, 1)

    def relay(dy, i, p):
        if i % 2 == 0:
            push2(3, dy, i, p, z_up, dy, 0)
        else:
            push2(1, dy, i, p, z_dn, dy, 0)

    def send_x(cb, target, n, rs):
        remote(xbuf.at[cb], xbuf.at[cb], x_send.at[n], rs, target).start()

    def x_got(dyl, dx):
        here = xbuf.at[at_col(dyl, dx)]
        remote(here, here, x_send.at[0], x_recv.at[dyl, dx], core_other).wait_recv()

    x_own.wait()
    send_x(c, (r, at_col(1, 0)), 0, x_recv.at[1, 0])
    for dx in (1, 2, 3):
        send_x(c, (r, at_col(0, dx)), dx, x_recv.at[0, NX - dx])

    for i in range(NCH):
        for cp in loads[i]:
            cp.wait()
        value = gbuf[i].astype(F32) * gelu_grad(vbuf[i].astype(F32))
        panel[i, 2 * z + yh, pl.ds(pl.multiple_of(k * tb, tb), tb), :] = value.astype(BF16)
        push(0, 0, i, z_up, 3, 0, 0)
        push(0, 0, i, z_dn, 1, 0, 0)
        push(0, 0, i, y_other, 0, 1, 0)
        share(0, 0, i)

    w_loads = []
    for i in range(NCH):
        cols = pl.ds(i * cw, cw)
        cp = pltpu.make_async_copy(w_hbm.at[:, cols], wbuf.at[i], w_sem.at[i])
        cp.start()
        w_loads.append(cp)

    def packed(values, step):
        def word(part):
            w = sum(v << (2 * n) for n, v in enumerate(part))
            return jnp.int32(w - (1 << 32) if w >> 31 else w)

        w = jnp.where(step < 16, word(values[:16]), word(values[16:]))
        return lax.shift_right_arithmetic(w, 2 * lax.rem(step, 16)) & 3

    def unit(units, step):
        return packed([u[0] if u else 0 for u in units], step), packed([u[1] if u else 0 for u in units], step)

    def pair(kind):
        def of(own, near, cross, far):
            return jnp.where(kind < 2, jnp.where(kind == 0, own, near), jnp.where(kind == 2, cross, far))

        first = of(2 * z, owned(3, 0), owned(3, 1), 2 * lax.rem(z + 2, NZ))
        second = of(2 * z + 1, owned(1, 0), owned(1, 1), 2 * lax.rem(z + 2, NZ) + 1)
        return first, second

    def busy(units, step):
        return packed([0 if u is None else 1 for u in units], step) == 1

    def choose(step, what, lo, hi):
        if hi - lo == 1:
            what(lo)
        else:
            mid = (lo + hi) // 2
            lax.cond(
                step < mid, lambda: choose(step, what, lo, mid), lambda: choose(step, what, mid, hi)
            )

    def mm1(step):
        kind, group = unit(MM1, step)
        blocks = pair(kind)
        term = None
        for j in range(2):
            i = 2 * group + j
            left = jnp.concatenate([panel[i, cb] for cb in blocks], axis=0)
            d = lax.dot_general(left, wbuf[i], NT, preferred_element_type=F32)
            term = d if term is None else term + d
        for n, cb in enumerate(blocks):
            acc[cb] = acc[cb] + term[n * ob:(n + 1) * ob]

    def mm1h(step):
        p, group = unit(MM1H, step)
        plane = lax.rem(z + 2, NZ)
        term = None
        for j in range(2):
            i = 2 * group + j
            rows = [
                panel[i, 2 * plane + q // 2, pl.ds(pl.multiple_of(q % 2 * tb + p * hb, hb), hb), :] for q in range(4)
            ]
            d = lax.dot_general(jnp.concatenate(rows, axis=0), wbuf[i], NT, preferred_element_type=F32)
            term = d if term is None else term + d
        acc2[p] = acc2[p] + term

    def mm2(step):
        kind, group = unit(MM2, step)
        blocks = pair(kind)
        left = jnp.concatenate([xt[cb] for cb in blocks], axis=1)
        for j in range(2):
            i = 2 * group + j
            right = jnp.concatenate([panel[i, cb] for cb in blocks], axis=0)
            d = lax.dot_general(left, right, NN, preferred_element_type=F32)
            dw_ref[i] = dw_ref[i] + d

    def sib(kind, group):
        offsets = {OWN: ((0, 0), (0, 1)), NEAR: ((3, 0), (1, 0)), CROSS: ((3, 1), (1, 1))}[kind]
        for dz, dy in offsets:
            for i in GROUPS[group]:
                got(dz, dy, 1, i)

    def sib2(p, group):
        for dy in range(2):
            for i in GROUPS[group]:
                got2(dy, 1, i, p)

    def quarter(plane, xc):
        near = xc // 2 == lax.rem(plane, 2)
        side = jnp.where(near, lax.rem(xc, 2), 1 - lax.rem(xc, 2))
        return 2 * plane + side, pl.multiple_of(jnp.where(near, 0, tb), tb)

    def rs_copy(dz, dx):
        plane = lax.rem(z + dz, NZ)
        cb, row = quarter(plane, lax.rem(x + dx, NX))
        return remote(
            sbuf.at[cb, pl.ds(row, tb), :], rx.at[dz, dx - 1], rs_send.at[dz, dx - 1], rs_recv.at[dz, dx - 1],
            (r, at_col(0, dx)),
        )

    def rs_start(dz):
        plane = lax.rem(z + dz, NZ)
        for h in range(2):
            sbuf[2 * plane + h] = acc[2 * plane + h].astype(BF16)
        for dx in (1, 2, 3):
            rs_copy(dz, dx).start()

    def own_copy(dz, p=None):
        plane = lax.rem(z + dz, NZ)
        near = x // 2 == lax.rem(plane, 2)
        j = jnp.where(near, 0, 1)
        owner_x = jnp.where(near, x, 3 - x)
        owner_yl = plane // 2
        rel = lax.rem(owner_yl + yl, 2)
        src, dst, sem = stage.at[dz], parts.at[j, rel], own_send.at[dz]
        if p is not None:
            part = pl.ds(p * hb, hb)
            src, dst, sem = stage.at[dz, part, :], parts.at[j, rel, part, :], own2_send.at[p]
        cp = remote(src, dst, sem, own_recv.at[j, rel], (r, owner_yl * NX + owner_x))
        return cp, jnp.logical_or(owner_x != x, owner_yl != yl)

    def rs_collect(dz):
        plane = lax.rem(z + dz, NZ)
        cb, row = quarter(plane, x)
        total = acc[cb, pl.ds(row, tb), :]
        for dx in (1, 2, 3):
            rs_copy(dz, dx).wait_recv()
            total = total + rx[dz, dx - 1].astype(F32)
        stage[dz] = total.astype(BF16)
        cp, away = own_copy(dz)
        pl.when(away)(cp.start)

    def rs2_copy(p, dx):
        plane = lax.rem(z + 2, NZ)
        cb, row = quarter(plane, lax.rem(x + dx, NX))
        return remote(
            sbuf.at[cb, pl.ds(pl.multiple_of(row + p * hb, hb), hb), :], rx.at[2, dx - 1, pl.ds(p * hb, hb), :],
            rs2_send.at[p, dx - 1], rs2_recv.at[p, dx - 1], (r, at_col(0, dx)),
        )

    def rs2_start(p):
        plane = lax.rem(z + 2, NZ)
        for q in range(4):
            row = q % 2 * tb + p * hb
            sbuf[2 * plane + q // 2, row:row + hb, :] = acc2[p, q * hb:(q + 1) * hb, :].astype(BF16)
        for dx in (1, 2, 3):
            rs2_copy(p, dx).start()

    def rs2_collect(p):
        plane = lax.rem(z + 2, NZ)
        cb, row = quarter(plane, x)
        row = lax.rem(cb, 2) * tb + row // 2
        total = acc2[p, pl.ds(pl.multiple_of(row, hb), hb), :]
        for dx in (1, 2, 3):
            rs2_copy(p, dx).wait_recv()
            total = total + rx[2, dx - 1, p * hb:(p + 1) * hb, :].astype(F32)
        stage[2, p * hb:(p + 1) * hb, :] = total.astype(BF16)
        cp, away = own_copy(2, p)
        pl.when(away)(cp.start)

    def rs_finish():
        mine = lax.rem(c // 2 - z + NZ, NZ)
        for j in range(2):
            for rel in range(2):
                if j or rel:
                    here = parts.at[j, rel]
                    remote(here, here, own_send.at[0], own_recv.at[j, rel], core_other).wait_recv()
            first = parts[1, 0] if j else stage[mine]
            total = first.astype(F32) + parts[j, 1].astype(F32)
            gi_ref[j * tb:(j + 1) * tb, :] = total.astype(gi_ref.dtype)

    def near(i):
        for dz in (3, 1):
            got(dz, 0, 0, i)
            if i >= NA:
                push(dz, 0, i, y_other, dz, 1, 0)
            share(dz, 0, i)

    def other(i):
        got(0, 1, 0, i)
        if i < NA:
            push(0, 1, i, z_up, 3, 1, 0)
            push(0, 1, i, z_dn, 1, 1, 0)
        share(0, 1, i)

    def near_other(i):
        for dz in (3, 1):
            got(dz, 1, 0, i)
            share(dz, 1, i)
        if i < NA:
            relay(1, i, 0)

    def far(i, p):
        got2(0, 0, i, p)
        if i >= NA:
            push2(2, 0, i, p, y_other, 1, 0)
        push2(2, 0, i, p, core_other, 0, 1)

    def far_other(i, p):
        got2(1, 0, i, p)
        push2(2, 1, i, p, core_other, 1, 1)

    def forward_x():
        x_got(1, 0)
        for dx in (1, 2, 3):
            send_x(at_col(1, 0), (r, at_col(0, dx)), 3 + dx, x_recv.at[1, NX - dx])

    def clear(chunks):
        for i in chunks:
            dw_ref[i] = jnp.zeros_like(dw_ref[i])

    def before(n):
        if n == 0:
            acc[...] = jnp.zeros_like(acc)
            acc2[...] = jnp.zeros_like(acc2)
            near(0)
            forward_x()
            clear((0, 1))
            near(1)
            for cp in w_loads:
                cp.wait()
        if n == 1:
            other(0)
            near(2)
            other(1)
            clear((2, 3))
        if n == 2:
            near(3)
            other(2)
        if n == 3:
            near(4)
            other(3)
            clear((4, 5))
        if n == 4:
            near(5)
            for i in (4, 5):
                for p in range(2):
                    relay(0, i, p)
            for i in range(NA):
                relay(0, i, 0)
        if n == 6:
            near_other(0)
        if n == 7:
            near_other(1)
        if n == 8:
            other(4)
            other(5)
            near_other(2)
        if n == 9:
            near_other(3)
            for dy in range(2):
                for i in range(NA):
                    relay(dy, i, 1)
        if n == 10:
            near_other(4)
        if n == 11:
            near_other(5)
            for p in range(2):
                far(4, p)
                far(5, p)
            for i in range(NA):
                far(i, 0)
        if n == 12:
            far_other(2, 0)
            far_other(3, 0)
        if n == 13:
            far_other(4, 0)
            far_other(5, 0)
        if n == 14:
            for i in range(NA):
                far(i, 1)
        if n == 15:
            far_other(0, 1)
            far_other(1, 1)
        if n == 16:
            far_other(2, 1)
            far_other(3, 1)
        if MM1[n] is not None:
            sib(*MM1[n])
        if MM1H[n] is not None:
            sib2(*MM1H[n])
        if n == 13:
            rs_collect(0)
        if n == 19:
            rs2_collect(0)
        if n == 20:
            rs2_collect(1)

    def between(n):
        if n == 4:
            for dyl in range(2):
                for dx in (1, 2, 3):
                    x_got(dyl, dx)
            for cb in range(2 * NZ):
                xt[cb] = xbuf[cb].T
        if n == 9:
            rs_start(0)
        if n == 11:
            rs_start(3)
            rs_start(1)
            far_other(0, 0)
            far_other(1, 0)
        if n == 14:
            rs2_start(0)
            far_other(4, 1)
            far_other(5, 1)
        if n == 16:
            rs_collect(3)
        if n == 17:
            rs2_start(1)
            rs_collect(1)

    @pl.loop(0, STEPS)
    def _(step):
        choose(step, before, 0, STEPS)
        pl.when(busy(MM1, step))(lambda: mm1(step))
        pl.when(busy(MM1H, step))(lambda: mm1h(step))
        choose(step, between, 0, STEPS)
        pl.when(busy(MM2, step))(lambda: mm2(step))

    rs_finish()

    assert n_sent[0] == N_SENDS and n_sent2[0] == N_SENDS2
    for n in range(N_SENDS):
        here = block(0, 0, 0, 0)
        remote(here, here, send_sem.at[n], recv_sem.at[0, 0, 0, 0], core_other).wait_send()
    for n in range(N_SENDS2):
        here = half(0, 0, 0, 0, 0)
        remote(here, here, send_sem.at[N_SENDS + n], recv_sem.at[0, 0, 0, 0], core_other).wait_send()
    for n in range(7):
        remote(xbuf.at[c], xbuf.at[c], x_send.at[n], x_recv.at[0, 0], core_other).wait_send()
    for dz in (0, 3, 1):
        for dx in (1, 2, 3):
            rs_copy(dz, dx).wait_send()
        cp, away = own_copy(dz)
        pl.when(away)(cp.wait_send)
    for p in range(2):
        for dx in (1, 2, 3):
            rs2_copy(p, dx).wait_send()
        cp, away = own_copy(2, p)
        pl.when(away)(cp.wait_send)


N_SENDS = (12 + 8) + (6 + 4) + 36
N_SENDS2 = 20 + 4 + 24


def out_kernel(gi_ref, dw_ref, gi_out, dw_out, buf, sem):
    cw = dw_ref.shape[2]
    gi_copy = pltpu.make_async_copy(gi_ref, gi_out, sem.at[NCH])
    gi_copy.start()
    copies = []
    for i in range(NCH):
        buf[i] = dw_ref[i].astype(buf.dtype)
        cp = pltpu.make_async_copy(buf.at[i], dw_out.at[:, pl.ds(i * cw, cw)], sem.at[i])
        cp.start()
        copies.append(cp)
    for cp in copies:
        cp.wait()
    gi_copy.wait()


def body(grad_hidden, pre_act, inputs, weight):
    tb, ft = grad_hidden.shape
    ob, dt = inputs.shape
    cw = ft // NCH
    hbm = pl.BlockSpec(memory_space=pltpu.HBM)
    vmem = pl.BlockSpec(memory_space=pltpu.VMEM)
    dma = pltpu.SemaphoreType.DMA
    gi, dw = pl.pallas_call(
        main_kernel,
        out_shape=(pltpu.VMEM((ob, dt), BF16), pltpu.VMEM((NCH, dt, cw), F32)),
        in_specs=[hbm] * 4,
        out_specs=(vmem, vmem),
        scratch_shapes=[
            pltpu.VMEM((NCH, tb, cw), BF16),
            pltpu.VMEM((NCH, tb, cw), BF16),
            pltpu.VMEM((NCH, 8, ob, cw), BF16),
            pltpu.VMEM((NCH, dt, cw), BF16),
            pltpu.VMEM((8, ob, dt), BF16),
            pltpu.VMEM((8, dt, ob), BF16),
            pltpu.VMEM((8, ob, dt), F32),
            pltpu.VMEM((2, ob, dt), F32),
            pltpu.VMEM((8, ob, dt), BF16),
            pltpu.VMEM((NZ, NX - 1, tb, dt), BF16),
            pltpu.VMEM((NZ, tb, dt), BF16),
            pltpu.VMEM((2, 2, tb, dt), BF16),
            dma((2, NCH)),
            dma((NCH,)),
            dma,
            dma((N_SENDS + N_SENDS2,)),
            dma((2, 2, NZ, NCH)),
            dma((2, 2, NCH, 2)),
            dma((7,)),
            dma((2, NX)),
            dma((NZ, NX - 1)),
            dma((NZ, NX - 1)),
            dma((2, NX - 1)),
            dma((2, NX - 1)),
            dma((NZ,)),
            dma((2,)),
            dma((2, 2)),
        ],
        compiler_params=pltpu.CompilerParams(
            collective_id=0, has_side_effects=True, vmem_limit_bytes=44 * 2**20
        ),
        name="gather_and_multiply",
    )(grad_hidden, pre_act, inputs, weight)
    return pl.pallas_call(
        out_kernel,
        out_shape=(
            jax.ShapeDtypeStruct((ob, dt), BF16),
            jax.ShapeDtypeStruct((dt, ft), BF16),
        ),
        in_specs=[vmem, vmem],
        out_specs=(hbm, hbm),
        scratch_shapes=[pltpu.VMEM((NCH, dt, cw), BF16), dma((NCH + 1,))],
        compiler_params=pltpu.CompilerParams(vmem_limit_bytes=20 * 2**20),
        name="round_and_write",
    )(gi, dw)


def solution(mesh):
    return jax.shard_map(
        body,
        mesh=mesh,
        in_specs=(P("row", "col"), P("row", "col"), P("col", "row"), P("row", "col")),
        out_specs=(P("col", "row"), P("row", "col")),
        check_vma=False,
    )
```

time: 76.6 us -> 73 us (0.953)
  Pallas kernels: 75.8 us -> 72.3 us
    pallas_call x1, Pallas kernels: 72 us -> 68.4 us  [body(): pl.pallas_call(main_kernel, out_shape=(pltpu.VMEM((ob, dt), BF16), pltpu....]
where the time goes in v3:
time: 73 us; the launch traced here: 72.9 us
  Pallas kernels  72.3 us (99%)
    pallas_call x1, Pallas kernels, body(): pl.pallas_call(main_kernel, out_shape=(pltpu.VMEM((ob, dt), BF16), pltpu....  68.4 us
    pallas_call x1, Pallas kernels, body(): pl.pallas_call(out_kernel, out_shape=(jax.ShapeDtypeStruct((ob, dt), BF16...  3.86 us

profile of v3, /device:TPU:8, one launch (start us, length us, event | category | flops | bytes accessed | tf_op | source)
XLA Modules:
  0.0 72.9 jit_solution(8178057307238993096)
XLA Ops:
  0.6 68.4 %gather_and_multiply.1 = (bf16[128,768]{1,0:T(8,128)(2,1)S(1)}, f32[6,768,1024]{2,1,0:T(8,128)S(1)}) custom-call(bf16[64,6144]{1,0:T(8,128)(2,1)} %g_hbm.1, bf16[64,6144]{1,0:T(8,128)(2,1)} %v_hbm.1, bf16[128,768]{1,0:T(8,128)(2,1)} %x_hbm.1, bf16[768,6144]{1,0:T(8,128)(2,1)} %w_hbm.1), custom_call_target="tpu_custom_call" | custom-call | tf_op jit(solution)/shard_map/gather_and_multiply/pallas_call | solution.py:535
  69.1 3.9 %round_and_write.1 = (bf16[128,768]{1,0:T(8,128)(2,1)}, bf16[768,6144]{1,0:T(8,128)(2,1)}) custom-call(bf16[128,768]{1,0:T(8,128)(2,1)S(1)} %get-tuple-element.4.gi_ref, f32[6,768,1024]{2,1,0:T(8,128)S(1)} %get-tuple-element.5.dw_ref), custom_call_target="tpu_custom_call" | custom-call | tf_op jit(solution)/shard_map/round_and_write/pallas_call | solution.py:574

commit v4 on v3

--- a/solution.py
+++ b/solution.py
@@ -17,21 +17,21 @@
     ((NEAR, 0), None, None),
     ((OWN, 0), None, None),
     ((NEAR, 1), None, None),
-    ((OWN, 1), None, None),
-    ((NEAR, 2), None, (OWN, 0)),
-    (None, None, (NEAR, 0)),
+    ((OWN, 1), None, (OWN, 0)),
+    ((NEAR, 2), None, (NEAR, 0)),
     (None, None, (OWN, 1)),
-    ((CROSS, 0), None, (NEAR, 1)),
-    (None, None, (NEAR, 2)),
+    (None, None, (NEAR, 1)),
+    ((CROSS, 0), None, (NEAR, 2)),
     ((OWN, 2), None, (OWN, 2)),
-    ((CROSS, 1), None, None),
-    ((CROSS, 2), None, (CROSS, 0)),
+    (None, None, (CROSS, 0)),
+    ((CROSS, 1), None, (CROSS, 1)),
+    ((CROSS, 2), None, (CROSS, 2)),
     (None, (0, 0), None),
     (None, (0, 1), None),
-    (None, (0, 2), (CROSS, 1)),
+    (None, (0, 2), None),
     (None, (1, 2), None),
     (None, (1, 0), None),
-    (None, (1, 1), (CROSS, 2)),
+    (None, (1, 1), None),
     (None, None, (FAR, 2)),
     (None, None, (FAR, 0)),
     (None, None, (FAR, 1)),
@@ -58,7 +58,7 @@
     gi_ref, dw_ref,
     gbuf, vbuf, panel, wbuf, xbuf, xt, acc, acc2, sbuf, rx, stage, parts,
     load_sem, w_sem, x_own_sem, send_sem, recv_sem, far_sem, x_send, x_recv, rs_send, rs_recv, rs2_send, rs2_recv,
-    own_send, own2_send, own_recv,
+    own_send, own_recv,
 ):
     r = lax.axis_index("row")
     c = lax.axis_index("col")
@@ -94,6 +94,14 @@
     partners += [(r, at_col(0, dx)) for dx in (1, 2, 3)]
     for partner in partners:
         pl.semaphore_signal(barrier, inc=1, device_id=partner, device_id_type=pl.DeviceIdType.MESH)
+
+    def grad_pre(i):
+        for cp in loads[i]:
+            cp.wait()
+        value = gbuf[i].astype(F32) * gelu_grad(vbuf[i].astype(F32))
+        panel[i, 2 * z + yh, pl.ds(pl.multiple_of(k * tb, tb), tb), :] = value.astype(BF16)
+
+    grad_pre(0)
     pl.semaphore_wait(barrier, len(partners))
 
     hb = tb // 2
@@ -157,10 +165,8 @@
         send_x(c, (r, at_col(0, dx)), dx, x_recv.at[0, NX - dx])
 
     for i in range(NCH):
-        for cp in loads[i]:
-            cp.wait()
-        value = gbuf[i].astype(F32) * gelu_grad(vbuf[i].astype(F32))
-        panel[i, 2 * z + yh, pl.ds(pl.multiple_of(k * tb, tb), tb), :] = value.astype(BF16)
+        if i:
+            grad_pre(i)
         push(0, 0, i, z_up, 3, 0, 0)
         push(0, 0, i, z_dn, 1, 0, 0)
         push(0, 0, i, y_other, 0, 1, 0)
@@ -250,56 +256,53 @@
             for i in GROUPS[group]:
                 got2(dy, 1, i, p)
 
-    def quarter(plane, xc):
-        near = xc // 2 == lax.rem(plane, 2)
-        side = jnp.where(near, lax.rem(xc, 2), 1 - lax.rem(xc, 2))
-        return 2 * plane + side, pl.multiple_of(jnp.where(near, 0, tb), tb)
-
-    def rs_copy(dz, dx):
-        plane = lax.rem(z + dz, NZ)
-        cb, row = quarter(plane, lax.rem(x + dx, NX))
+    def quarter(kind, xc):
+        near = xc // 2 == lax.rem(z + (kind in (NEAR, CROSS)), 2)
+        h = jnp.where(near, lax.rem(xc, 2), 1 - lax.rem(xc, 2))
+        row = pl.multiple_of(jnp.where(near, 0, tb), tb)
+        if kind in (OWN, FAR):
+            return 2 * lax.rem(z + kind // FAR * 2, NZ) + h, row
+        dy = kind - NEAR
+        return jnp.where(h == lax.rem(yh + dy, 2), owned(3, dy), owned(1, dy)), row
+
+    def rs_copy(kind, dx):
+        cb, row = quarter(kind, lax.rem(x + dx, NX))
         return remote(
-            sbuf.at[cb, pl.ds(row, tb), :], rx.at[dz, dx - 1], rs_send.at[dz, dx - 1], rs_recv.at[dz, dx - 1],
+            sbuf.at[cb, pl.ds(row, tb), :], rx.at[kind, dx - 1], rs_send.at[kind, dx - 1], rs_recv.at[kind, dx - 1],
             (r, at_col(0, dx)),
         )
 
-    def rs_start(dz):
-        plane = lax.rem(z + dz, NZ)
-        for h in range(2):
-            sbuf[2 * plane + h] = acc[2 * plane + h].astype(BF16)
+    def rs_start(kind):
+        blocks = (2 * z, 2 * z + 1) if kind == OWN else (owned(3, kind - NEAR), owned(1, kind - NEAR))
+        for cb in blocks:
+            sbuf[cb] = acc[cb].astype(BF16)
         for dx in (1, 2, 3):
-            rs_copy(dz, dx).start()
-
-    def own_copy(dz, p=None):
-        plane = lax.rem(z + dz, NZ)
-        near = x // 2 == lax.rem(plane, 2)
-        j = jnp.where(near, 0, 1)
-        owner_x = jnp.where(near, x, 3 - x)
-        owner_yl = plane // 2
+            rs_copy(kind, dx).start()
+
+    def to_owner(src, rows, s_sem, cb, j):
+        owner_yl, owner_x = cb // NX, lax.rem(cb, NX)
         rel = lax.rem(owner_yl + yl, 2)
-        src, dst, sem = stage.at[dz], parts.at[j, rel], own_send.at[dz]
-        if p is not None:
-            part = pl.ds(p * hb, hb)
-            src, dst, sem = stage.at[dz, part, :], parts.at[j, rel, part, :], own2_send.at[p]
-        cp = remote(src, dst, sem, own_recv.at[j, rel], (r, owner_yl * NX + owner_x))
+        cp = remote(src, parts.at[j, rel, rows, :], s_sem, own_recv.at[j, rel], (r, owner_yl * NX + owner_x))
         return cp, jnp.logical_or(owner_x != x, owner_yl != yl)
 
-    def rs_collect(dz):
-        plane = lax.rem(z + dz, NZ)
-        cb, row = quarter(plane, x)
+    def own_copy(kind):
+        cb, row = quarter(kind, x)
+        return to_owner(stage.at[kind], pl.ds(0, tb), own_send.at[kind], cb, row // tb)
+
+    def rs_collect(kind):
+        cb, row = quarter(kind, x)
         total = acc[cb, pl.ds(row, tb), :]
         for dx in (1, 2, 3):
-            rs_copy(dz, dx).wait_recv()
-            total = total + rx[dz, dx - 1].astype(F32)
-        stage[dz] = total.astype(BF16)
-        cp, away = own_copy(dz)
+            rs_copy(kind, dx).wait_recv()
+            total = total + rx[kind, dx - 1].astype(F32)
+        stage[kind] = total.astype(BF16)
+        cp, away = own_copy(kind)
         pl.when(away)(cp.start)
 
     def rs2_copy(p, dx):
-        plane = lax.rem(z + 2, NZ)
-        cb, row = quarter(plane, lax.rem(x + dx, NX))
+        cb, row = quarter(FAR, lax.rem(x + dx, NX))
         return remote(
-            sbuf.at[cb, pl.ds(pl.multiple_of(row + p * hb, hb), hb), :], rx.at[2, dx - 1, pl.ds(p * hb, hb), :],
+            sbuf.at[cb, pl.ds(pl.multiple_of(row + p * hb, hb), hb), :], rx.at[FAR, dx - 1, pl.ds(p * hb, hb), :],
             rs2_send.at[p, dx - 1], rs2_recv.at[p, dx - 1], (r, at_col(0, dx)),
         )
 
@@ -311,27 +314,41 @@
         for dx in (1, 2, 3):
             rs2_copy(p, dx).start()
 
+    def own2_copy(p):
+        cb, row = quarter(FAR, x)
+        part = pl.ds(p * hb, hb)
+        return to_owner(stage.at[FAR, part, :], part, own_send.at[FAR + p], cb, row // tb)
+
     def rs2_collect(p):
-        plane = lax.rem(z + 2, NZ)
-        cb, row = quarter(plane, x)
+        cb, row = quarter(FAR, x)
         row = lax.rem(cb, 2) * tb + row // 2
         total = acc2[p, pl.ds(pl.multiple_of(row, hb), hb), :]
         for dx in (1, 2, 3):
             rs2_copy(p, dx).wait_recv()
-            total = total + rx[2, dx - 1, p * hb:(p + 1) * hb, :].astype(F32)
-        stage[2, p * hb:(p + 1) * hb, :] = total.astype(BF16)
-        cp, away = own_copy(2, p)
+            total = total + rx[FAR, dx - 1, p * hb:(p + 1) * hb, :].astype(F32)
+        stage[FAR, p * hb:(p + 1) * hb, :] = total.astype(BF16)
+        cp, away = own2_copy(p)
         pl.when(away)(cp.start)
 
     def rs_finish():
-        mine = lax.rem(c // 2 - z + NZ, NZ)
+        offset = lax.rem(c // 2 - z + NZ, NZ)
+        beside = NEAR + lax.rem(lax.rem(c, 2) + yh, 2)
+        mine = jnp.where(offset == 0, OWN, jnp.where(offset == 2, FAR, beside))
+
+        def arrived(j, rel):
+            here = parts.at[j, rel]
+            remote(here, here, own_send.at[0], own_recv.at[j, rel], core_other).wait_recv()
+
+        def keep():
+            parts[0, 0] = stage[mine]
+
+        pl.when(offset == 1)(lambda: arrived(0, 0))
+        pl.when(offset != 1)(keep)
         for j in range(2):
             for rel in range(2):
                 if j or rel:
-                    here = parts.at[j, rel]
-                    remote(here, here, own_send.at[0], own_recv.at[j, rel], core_other).wait_recv()
-            first = parts[1, 0] if j else stage[mine]
-            total = first.astype(F32) + parts[j, 1].astype(F32)
+                    arrived(j, rel)
+            total = parts[j, 0].astype(F32) + parts[j, 1].astype(F32)
             gi_ref[j * tb:(j + 1) * tb, :] = total.astype(gi_ref.dtype)
 
     def near(i):
@@ -396,44 +413,25 @@
             near(4)
             other(3)
             clear((4, 5))
-        if n == 4:
-            near(5)
-            for i in (4, 5):
-                for p in range(2):
-                    relay(0, i, p)
-            for i in range(NA):
-                relay(0, i, 0)
         if n == 6:
-            near_other(0)
+            near_other(1)
         if n == 7:
-            near_other(1)
-        if n == 8:
             other(4)
             other(5)
+        if n == 8:
             near_other(2)
         if n == 9:
             near_other(3)
             for dy in range(2):
                 for i in range(NA):
                     relay(dy, i, 1)
-        if n == 10:
             near_other(4)
-        if n == 11:
-            near_other(5)
-            for p in range(2):
-                far(4, p)
-                far(5, p)
-            for i in range(NA):
-                far(i, 0)
         if n == 12:
             far_other(2, 0)
             far_other(3, 0)
         if n == 13:
             far_other(4, 0)
             far_other(5, 0)
-        if n == 14:
-            for i in range(NA):
-                far(i, 1)
         if n == 15:
             far_other(0, 1)
             far_other(1, 1)
@@ -445,35 +443,51 @@
         if MM1H[n] is not None:
             sib2(*MM1H[n])
         if n == 13:
-            rs_collect(0)
+            rs_collect(NEAR)
+            rs_collect(OWN)
+        if n == 15:
+            rs_collect(CROSS)
         if n == 19:
             rs2_collect(0)
-        if n == 20:
-            rs2_collect(1)
 
     def between(n):
-        if n == 4:
+        if n == 3:
+            near(5)
+            for i in (4, 5):
+                for p in range(2):
+                    relay(0, i, p)
+            for i in range(NA):
+                relay(0, i, 0)
             for dyl in range(2):
                 for dx in (1, 2, 3):
                     x_got(dyl, dx)
             for cb in range(2 * NZ):
                 xt[cb] = xbuf[cb].T
-        if n == 9:
-            rs_start(0)
+        if n == 4:
+            rs_start(NEAR)
+            near_other(0)
+        if n == 8:
+            rs_start(OWN)
+        if n == 10:
+            near_other(5)
+            for p in range(2):
+                far(4, p)
+                far(5, p)
         if n == 11:
-            rs_start(3)
-            rs_start(1)
+            rs_start(CROSS)
+            for i in range(NA):
+                far(i, 0)
             far_other(0, 0)
             far_other(1, 0)
+        if n == 13:
+            for i in range(NA):
+                far(i, 1)
+            far_other(4, 1)
+            far_other(5, 1)
         if n == 14:
             rs2_start(0)
-            far_other(4, 1)
-            far_other(5, 1)
-        if n == 16:
-            rs_collect(3)
         if n == 17:
             rs2_start(1)
-            rs_collect(1)
 
     @pl.loop(0, STEPS)
     def _(step):
@@ -483,6 +497,7 @@
         choose(step, between, 0, STEPS)
         pl.when(busy(MM2, step))(lambda: mm2(step))
 
+    rs2_collect(1)
     rs_finish()
 
     assert n_sent[0] == N_SENDS and n_sent2[0] == N_SENDS2
@@ -494,15 +509,16 @@
         remote(here, here, send_sem.at[N_SENDS + n], recv_sem.at[0, 0, 0, 0], core_other).wait_send()
     for n in range(7):
         remote(xbuf.at[c], xbuf.at[c], x_send.at[n], x_recv.at[0, 0], core_other).wait_send()
-    for dz in (0, 3, 1):
+    last = []
+    for kind in (OWN, NEAR, CROSS):
         for dx in (1, 2, 3):
-            rs_copy(dz, dx).wait_send()
-        cp, away = own_copy(dz)
-        pl.when(away)(cp.wait_send)
+            rs_copy(kind, dx).wait_send()
+        last.append(own_copy(kind))
     for p in range(2):
         for dx in (1, 2, 3):
             rs2_copy(p, dx).wait_send()
-        cp, away = own_copy(2, p)
+        last.append(own2_copy(p))
+    for cp, away in last:
         pl.when(away)(cp.wait_send)
 
 
@@ -547,8 +563,8 @@
             pltpu.VMEM((8, ob, dt), F32),
             pltpu.VMEM((2, ob, dt), F32),
             pltpu.VMEM((8, ob, dt), BF16),
-            pltpu.VMEM((NZ, NX - 1, tb, dt), BF16),
-            pltpu.VMEM((NZ, tb, dt), BF16),
+            pltpu.VMEM((4, NX - 1, tb, dt), BF16),
+            pltpu.VMEM((4, tb, dt), BF16),
             pltpu.VMEM((2, 2, tb, dt), BF16),
             dma((2, NCH)),
             dma((NCH,)),
@@ -558,12 +574,11 @@
             dma((2, 2, NCH, 2)),
             dma((7,)),
             dma((2, NX)),
-            dma((NZ, NX - 1)),
-            dma((NZ, NX - 1)),
+            dma((3, NX - 1)),
+            dma((3, NX - 1)),
             dma((2, NX - 1)),
             dma((2, NX - 1)),
-            dma((NZ,)),
-            dma((2,)),
+            dma((5,)),
             dma((2, 2)),
         ],
         compiler_params=pltpu.CompilerParams(

time: 73 us -> 72.5 us (level)
  no operation moved by 1% of the time
where the time goes in v4:
time: 72.5 us; the launch traced here: 72.3 us
  Pallas kernels  71.7 us (99%)
    pallas_call x1, Pallas kernels, body(): pl.pallas_call(main_kernel, out_shape=(pltpu.VMEM((ob, dt), BF16), pltpu....  67.8 us
    pallas_call x1, Pallas kernels, body(): pl.pallas_call(out_kernel, out_shape=(jax.ShapeDtypeStruct((ob, dt), BF16...  3.86 us

profile of v4, /device:TPU:8, one launch (start us, length us, event | category | flops | bytes accessed | tf_op | source)
XLA Modules:
  0.0 72.3 jit_solution(4948407364683219872)
XLA Ops:
  0.6 67.8 %gather_and_multiply.1 = (bf16[128,768]{1,0:T(8,128)(2,1)S(1)}, f32[6,768,1024]{2,1,0:T(8,128)S(1)}) custom-call(bf16[64,6144]{1,0:T(8,128)(2,1)} %g_hbm.1, bf16[64,6144]{1,0:T(8,128)(2,1)} %v_hbm.1, bf16[128,768]{1,0:T(8,128)(2,1)} %x_hbm.1, bf16[768,6144]{1,0:T(8,128)(2,1)} %w_hbm.1), custom_call_target="tpu_custom_call" | custom-call | tf_op jit(solution)/shard_map/gather_and_multiply/pallas_call | solution.py:551
  68.5 3.9 %round_and_write.1 = (bf16[128,768]{1,0:T(8,128)(2,1)}, bf16[768,6144]{1,0:T(8,128)(2,1)}) custom-call(bf16[128,768]{1,0:T(8,128)(2,1)S(1)} %get-tuple-element.4.gi_ref, f32[6,768,1024]{2,1,0:T(8,128)S(1)} %get-tuple-element.5.dw_ref), custom_call_target="tpu_custom_call" | custom-call | tf_op jit(solution)/shard_map/round_and_write/pallas_call | solution.py:589

commit v5 on v4

--- a/solution.py
+++ b/solution.py
@@ -56,9 +56,9 @@
 def main_kernel(
     g_hbm, v_hbm, x_hbm, w_hbm,
     gi_ref, dw_ref,
-    gbuf, vbuf, panel, wbuf, xbuf, xt, acc, acc2, sbuf, rx, stage, parts,
-    load_sem, w_sem, x_own_sem, send_sem, recv_sem, far_sem, x_send, x_recv, rs_send, rs_recv, rs2_send, rs2_recv,
-    own_send, own_recv,
+    gvbuf, panel, wbuf, xbuf, xt, acc, acc2, sbuf, rx, stage, parts,
+    load_sem, w_sem, x_own_sem, send_sem, recv_sem, far_sem, core_sem, core2_sem, x_send, x_recv, rs_send, rs_recv,
+    rs2_recv, own_send, own_recv,
 ):
     r = lax.axis_index("row")
     c = lax.axis_index("col")
@@ -79,16 +79,10 @@
 
     x_own = pltpu.make_async_copy(x_hbm, xbuf.at[c], x_own_sem)
     x_own.start()
-    loads = []
     for i in range(NCH):
         cols = pl.ds(i * cw, cw)
-        pair = (
-            pltpu.make_async_copy(g_hbm.at[:, cols], gbuf.at[i], load_sem.at[0, i]),
-            pltpu.make_async_copy(v_hbm.at[:, cols], vbuf.at[i], load_sem.at[1, i]),
-        )
-        for cp in pair:
-            cp.start()
-        loads.append(pair)
+        for n, src in enumerate((g_hbm, v_hbm)):
+            pltpu.make_async_copy(src.at[:, cols], gvbuf.at[i, n], load_sem.at[min(i, 1)]).start()
     barrier = pltpu.get_barrier_semaphore()
     partners = [z_up, z_dn, y_other, core_other, (r, at_col(1, 0))]
     partners += [(r, at_col(0, dx)) for dx in (1, 2, 3)]
@@ -96,9 +90,10 @@
         pl.semaphore_signal(barrier, inc=1, device_id=partner, device_id_type=pl.DeviceIdType.MESH)
 
     def grad_pre(i):
-        for cp in loads[i]:
-            cp.wait()
-        value = gbuf[i].astype(F32) * gelu_grad(vbuf[i].astype(F32))
+        if i < 2:
+            part = gvbuf.at[pl.ds(0, 1) if i == 0 else pl.ds(1, NCH - 1)]
+            pltpu.make_async_copy(part, part, load_sem.at[i]).wait()
+        value = gvbuf[i, 0].astype(F32) * gelu_grad(gvbuf[i, 1].astype(F32))
         panel[i, 2 * z + yh, pl.ds(pl.multiple_of(k * tb, tb), tb), :] = value.astype(BF16)
 
     grad_pre(0)
@@ -125,59 +120,61 @@
         rows = pl.ds(pl.multiple_of(lax.rem(k + dk, 2) * tb + p * hb, hb), hb)
         return panel.at[i, owned(dz, dy), rows, :]
 
-    def push(dz, dy, i, target, rz, ry, rk):
+    def push(dz, dy, i, target, sem):
         here = block(dz, dy, 0, i)
-        remote(here, here, send_sem.at[n_sent[0]], recv_sem.at[rk, ry, rz, i], target).start()
+        s_sem = send_sem.at[0 if n_sent[0] < FIRST_SENDS else 1]
+        remote(here, here, s_sem, sem, target).start()
         n_sent[0] += 1
 
-    def push2(dz, dy, i, p, target, ry, rk):
+    def push2(dz, dy, i, p, target, sem):
         here = half(dz, dy, 0, i, p)
-        remote(here, here, send_sem.at[N_SENDS + n_sent2[0]], far_sem.at[rk, ry, i, p], target).start()
+        remote(here, here, send_sem.at[1], sem, target).start()
         n_sent2[0] += 1
 
-    def got(dz, dy, dk, i):
-        here = block(dz, dy, dk, i)
-        remote(here, here, send_sem.at[0], recv_sem.at[dk, dy, dz, i], core_other).wait_recv()
-
-    def got2(dy, dk, i, p):
-        here = half(2, dy, dk, i, p)
-        remote(here, here, send_sem.at[0], far_sem.at[dk, dy, i, p], core_other).wait_recv()
+    def took(ref, sem):
+        remote(ref, ref, send_sem.at[0], sem, core_other).wait_recv()
+
+    def blocks_of(n, m, rows):
+        return panel.at[pl.ds(0, n), pl.ds(0, m), pl.ds(0, rows), :]
 
     def share(dz, dy, i):
-        push(dz, dy, i, core_other, dz, dy, 1)
+        kind = OWN if dz == 0 else NEAR + dy
+        push(dz, dy, i, core_other, core_sem.at[kind, i // 2])
+
+    def share2(dy, i, p):
+        push2(2, dy, i, p, core_other, core2_sem.at[p, i // 2])
+
+    def far_slot(dy, i, p):
+        if dy:
+            return far_sem.at[3 + 3 * p + i // 2]
+        return far_sem.at[2 if i >= NA else p]
 
     def relay(dy, i, p):
         if i % 2 == 0:
-            push2(3, dy, i, p, z_up, dy, 0)
+            push2(3, dy, i, p, z_up, far_slot(dy, i, p))
         else:
-            push2(1, dy, i, p, z_dn, dy, 0)
-
-    def send_x(cb, target, n, rs):
-        remote(xbuf.at[cb], xbuf.at[cb], x_send.at[n], rs, target).start()
-
-    def x_got(dyl, dx):
-        here = xbuf.at[at_col(dyl, dx)]
-        remote(here, here, x_send.at[0], x_recv.at[dyl, dx], core_other).wait_recv()
+            push2(1, dy, i, p, z_dn, far_slot(dy, i, p))
+
+    def send_x(cb, target, rs):
+        remote(xbuf.at[cb], xbuf.at[cb], x_send, rs, target).start()
 
     x_own.wait()
-    send_x(c, (r, at_col(1, 0)), 0, x_recv.at[1, 0])
+    send_x(c, (r, at_col(1, 0)), x_recv.at[0])
     for dx in (1, 2, 3):
-        send_x(c, (r, at_col(0, dx)), dx, x_recv.at[0, NX - dx])
+        send_x(c, (r, at_col(0, dx)), x_recv.at[1])
 
     for i in range(NCH):
         if i:
             grad_pre(i)
-        push(0, 0, i, z_up, 3, 0, 0)
-        push(0, 0, i, z_dn, 1, 0, 0)
-        push(0, 0, i, y_other, 0, 1, 0)
+        push(0, 0, i, z_up, recv_sem.at[0, i])
+        push(0, 0, i, z_dn, recv_sem.at[0, i])
+        push(0, 0, i, y_other, recv_sem.at[2, i])
         share(0, 0, i)
 
-    w_loads = []
     for i in range(NCH):
         cols = pl.ds(i * cw, cw)
-        cp = pltpu.make_async_copy(w_hbm.at[:, cols], wbuf.at[i], w_sem.at[i])
+        cp = pltpu.make_async_copy(w_hbm.at[:, cols], wbuf.at[i], w_sem)
         cp.start()
-        w_loads.append(cp)
 
     def packed(values, step):
         def word(part):
@@ -246,15 +243,10 @@
             dw_ref[i] = dw_ref[i] + d
 
     def sib(kind, group):
-        offsets = {OWN: ((0, 0), (0, 1)), NEAR: ((3, 0), (1, 0)), CROSS: ((3, 1), (1, 1))}[kind]
-        for dz, dy in offsets:
-            for i in GROUPS[group]:
-                got(dz, dy, 1, i)
+        took(blocks_of(2, 2, tb), core_sem.at[kind, group])
 
     def sib2(p, group):
-        for dy in range(2):
-            for i in GROUPS[group]:
-                got2(dy, 1, i, p)
+        took(blocks_of(2, 2, hb), core2_sem.at[p, group])
 
     def quarter(kind, xc):
         near = xc // 2 == lax.rem(z + (kind in (NEAR, CROSS)), 2)
@@ -268,7 +260,7 @@
     def rs_copy(kind, dx):
         cb, row = quarter(kind, lax.rem(x + dx, NX))
         return remote(
-            sbuf.at[cb, pl.ds(row, tb), :], rx.at[kind, dx - 1], rs_send.at[kind, dx - 1], rs_recv.at[kind, dx - 1],
+            sbuf.at[cb, pl.ds(row, tb), :], rx.at[kind, dx - 1], rs_send, rs_recv.at[kind],
             (r, at_col(0, dx)),
         )
 
@@ -292,8 +284,8 @@
     def rs_collect(kind):
         cb, row = quarter(kind, x)
         total = acc[cb, pl.ds(row, tb), :]
+        took(rx.at[kind], rs_recv.at[kind])
         for dx in (1, 2, 3):
-            rs_copy(kind, dx).wait_recv()
             total = total + rx[kind, dx - 1].astype(F32)
         stage[kind] = total.astype(BF16)
         cp, away = own_copy(kind)
@@ -303,7 +295,7 @@
         cb, row = quarter(FAR, lax.rem(x + dx, NX))
         return remote(
             sbuf.at[cb, pl.ds(pl.multiple_of(row + p * hb, hb), hb), :], rx.at[FAR, dx - 1, pl.ds(p * hb, hb), :],
-            rs2_send.at[p, dx - 1], rs2_recv.at[p, dx - 1], (r, at_col(0, dx)),
+            rs_send, rs2_recv.at[p], (r, at_col(0, dx)),
         )
 
     def rs2_start(p):
@@ -323,8 +315,8 @@
         cb, row = quarter(FAR, x)
         row = lax.rem(cb, 2) * tb + row // 2
         total = acc2[p, pl.ds(pl.multiple_of(row, hb), hb), :]
+        took(rx.at[FAR, :, pl.ds(p * hb, hb), :], rs2_recv.at[p])
         for dx in (1, 2, 3):
-            rs2_copy(p, dx).wait_recv()
             total = total + rx[FAR, dx - 1, p * hb:(p + 1) * hb, :].astype(F32)
         stage[FAR, p * hb:(p + 1) * hb, :] = total.astype(BF16)
         cp, away = own2_copy(p)
@@ -352,40 +344,43 @@
             gi_ref[j * tb:(j + 1) * tb, :] = total.astype(gi_ref.dtype)
 
     def near(i):
+        took(blocks_of(1, 2, tb), recv_sem.at[0, i])
         for dz in (3, 1):
-            got(dz, 0, 0, i)
             if i >= NA:
-                push(dz, 0, i, y_other, dz, 1, 0)
+                push(dz, 0, i, y_other, recv_sem.at[1, i])
             share(dz, 0, i)
 
     def other(i):
-        got(0, 1, 0, i)
+        took(blocks_of(1, 1, tb), recv_sem.at[2, i])
         if i < NA:
-            push(0, 1, i, z_up, 3, 1, 0)
-            push(0, 1, i, z_dn, 1, 1, 0)
+            push(0, 1, i, z_up, recv_sem.at[1, i])
+            push(0, 1, i, z_dn, recv_sem.at[1, i])
         share(0, 1, i)
 
     def near_other(i):
+        took(blocks_of(1, 2, tb), recv_sem.at[1, i])
         for dz in (3, 1):
-            got(dz, 1, 0, i)
             share(dz, 1, i)
         if i < NA:
             relay(1, i, 0)
 
-    def far(i, p):
-        got2(0, 0, i, p)
-        if i >= NA:
-            push2(2, 0, i, p, y_other, 1, 0)
-        push2(2, 0, i, p, core_other, 0, 1)
-
-    def far_other(i, p):
-        got2(1, 0, i, p)
-        push2(2, 1, i, p, core_other, 1, 1)
+    def far(chunks, halves):
+        took(blocks_of(1, len(chunks) * len(halves), hb), far_slot(0, chunks[0], halves[0]))
+        for p in halves:
+            for i in chunks:
+                if i >= NA:
+                    push2(2, 0, i, p, y_other, far_slot(1, i, p))
+                share2(0, i, p)
+
+    def far_other(group, p):
+        took(blocks_of(1, 2, hb), far_slot(1, 2 * group, p))
+        for i in GROUPS[group]:
+            share2(1, i, p)
 
     def forward_x():
-        x_got(1, 0)
+        took(xbuf.at[pl.ds(0, 1)], x_recv.at[0])
         for dx in (1, 2, 3):
-            send_x(at_col(1, 0), (r, at_col(0, dx)), 3 + dx, x_recv.at[1, NX - dx])
+            send_x(at_col(1, 0), (r, at_col(0, dx)), x_recv.at[1])
 
     def clear(chunks):
         for i in chunks:
@@ -399,8 +394,7 @@
             forward_x()
             clear((0, 1))
             near(1)
-            for cp in w_loads:
-                cp.wait()
+            pltpu.make_async_copy(wbuf, wbuf, w_sem).wait()
         if n == 1:
             other(0)
             near(2)
@@ -427,23 +421,20 @@
                     relay(dy, i, 1)
             near_other(4)
         if n == 12:
+            far_other(1, 0)
+        if n == 13:
             far_other(2, 0)
-            far_other(3, 0)
-        if n == 13:
-            far_other(4, 0)
-            far_other(5, 0)
         if n == 15:
             far_other(0, 1)
+        if n == 16:
             far_other(1, 1)
-        if n == 16:
-            far_other(2, 1)
-            far_other(3, 1)
         if MM1[n] is not None:
             sib(*MM1[n])
         if MM1H[n] is not None:
             sib2(*MM1H[n])
-        if n == 13:
+        if n == 12:
             rs_collect(NEAR)
+        if n == 12:
             rs_collect(OWN)
         if n == 15:
             rs_collect(CROSS)
@@ -458,9 +449,7 @@
                     relay(0, i, p)
             for i in range(NA):
                 relay(0, i, 0)
-            for dyl in range(2):
-                for dx in (1, 2, 3):
-                    x_got(dyl, dx)
+            took(xbuf.at[pl.ds(0, 6)], x_recv.at[1])
             for cb in range(2 * NZ):
                 xt[cb] = xbuf[cb].T
         if n == 4:
@@ -470,20 +459,14 @@
             rs_start(OWN)
         if n == 10:
             near_other(5)
-            for p in range(2):
-                far(4, p)
-                far(5, p)
+            far((4, 5), (0, 1))
         if n == 11:
             rs_start(CROSS)
-            for i in range(NA):
-                far(i, 0)
+            far((0, 1, 2, 3), (0,))
             far_other(0, 0)
-            far_other(1, 0)
         if n == 13:
-            for i in range(NA):
-                far(i, 1)
-            far_other(4, 1)
-            far_other(5, 1)
+            far((0, 1, 2, 3), (1,))
+            far_other(2, 1)
         if n == 14:
             rs2_start(0)
         if n == 17:
@@ -501,29 +484,22 @@
     rs_finish()
 
     assert n_sent[0] == N_SENDS and n_sent2[0] == N_SENDS2
-    for n in range(N_SENDS):
-        here = block(0, 0, 0, 0)
-        remote(here, here, send_sem.at[n], recv_sem.at[0, 0, 0, 0], core_other).wait_send()
-    for n in range(N_SENDS2):
-        here = half(0, 0, 0, 0, 0)
-        remote(here, here, send_sem.at[N_SENDS + n], recv_sem.at[0, 0, 0, 0], core_other).wait_send()
-    for n in range(7):
-        remote(xbuf.at[c], xbuf.at[c], x_send.at[n], x_recv.at[0, 0], core_other).wait_send()
-    last = []
-    for kind in (OWN, NEAR, CROSS):
-        for dx in (1, 2, 3):
-            rs_copy(kind, dx).wait_send()
-        last.append(own_copy(kind))
-    for p in range(2):
-        for dx in (1, 2, 3):
-            rs2_copy(p, dx).wait_send()
-        last.append(own2_copy(p))
+    rest = 2 * (N_SENDS - FIRST_SENDS) + N_SENDS2
+    for sem, ref in (
+        (send_sem.at[0], blocks_of(NCH, FIRST_SENDS // NCH, tb)),
+        (send_sem.at[1], blocks_of(NCH, rest // 2 // NCH, tb)),
+        (x_send, xbuf.at[pl.ds(0, 7)]),
+        (rs_send, rx),
+    ):
+        remote(ref, ref, sem, recv_sem.at[0, 0], core_other).wait_send()
+    last = [own_copy(kind) for kind in (OWN, NEAR, CROSS)] + [own2_copy(p) for p in range(2)]
     for cp, away in last:
         pl.when(away)(cp.wait_send)
 
 
 N_SENDS = (12 + 8) + (6 + 4) + 36
 N_SENDS2 = 20 + 4 + 24
+FIRST_SENDS = 48
 
 
 def out_kernel(gi_ref, dw_ref, gi_out, dw_out, buf, sem):
@@ -554,8 +530,7 @@
         in_specs=[hbm] * 4,
         out_specs=(vmem, vmem),
         scratch_shapes=[
-            pltpu.VMEM((NCH, tb, cw), BF16),
-            pltpu.VMEM((NCH, tb, cw), BF16),
+            pltpu.VMEM((NCH, 2, tb, cw), BF16),
             pltpu.VMEM((NCH, 8, ob, cw), BF16),
             pltpu.VMEM((NCH, dt, cw), BF16),
             pltpu.VMEM((8, ob, dt), BF16),
@@ -566,18 +541,19 @@
             pltpu.VMEM((4, NX - 1, tb, dt), BF16),
             pltpu.VMEM((4, tb, dt), BF16),
             pltpu.VMEM((2, 2, tb, dt), BF16),
-            dma((2, NCH)),
-            dma((NCH,)),
+            dma((2,)),
             dma,
-            dma((N_SENDS + N_SENDS2,)),
-            dma((2, 2, NZ, NCH)),
-            dma((2, 2, NCH, 2)),
-            dma((7,)),
-            dma((2, NX)),
-            dma((3, NX - 1)),
-            dma((3, NX - 1)),
-            dma((2, NX - 1)),
-            dma((2, NX - 1)),
+            dma,
+            dma((2,)),
+            dma((3, NCH)),
+            dma((9,)),
+            dma((3, 3)),
+            dma((2, 3)),
+            dma,
+            dma((2,)),
+            dma,
+            dma((3,)),
+            dma((2,)),
             dma((5,)),
             dma((2, 2)),
         ],

time: 72.5 us -> 69.6 us (0.960)
  Pallas kernels: 71.7 us -> 68.8 us
    pallas_call x1, Pallas kernels: 67.8 us -> 65 us  [body(): pl.pallas_call(main_kernel, out_shape=(pltpu.VMEM((ob, dt), BF16), pltpu....]
where the time goes in v5:
time: 69.6 us; the launch traced here: 69.5 us
  Pallas kernels  68.8 us (99%)
    pallas_call x1, Pallas kernels, body(): pl.pallas_call(main_kernel, out_shape=(pltpu.VMEM((ob, dt), BF16), pltpu....  65 us
    pallas_call x1, Pallas kernels, body(): pl.pallas_call(out_kernel, out_shape=(jax.ShapeDtypeStruct((ob, dt), BF16...  3.86 us

profile of v5, /device:TPU:8, one launch (start us, length us, event | category | flops | bytes accessed | tf_op | source)
XLA Modules:
  0.0 69.5 jit_solution(3180181044062816694)
XLA Ops:
  0.6 65.0 %gather_and_multiply.1 = (bf16[128,768]{1,0:T(8,128)(2,1)S(1)}, f32[6,768,1024]{2,1,0:T(8,128)S(1)}) custom-call(bf16[64,6144]{1,0:T(8,128)(2,1)} %g_hbm.1, bf16[64,6144]{1,0:T(8,128)(2,1)} %v_hbm.1, bf16[128,768]{1,0:T(8,128)(2,1)} %x_hbm.1, bf16[768,6144]{1,0:T(8,128)(2,1)} %w_hbm.1), custom_call_target="tpu_custom_call" | custom-call | tf_op jit(solution)/shard_map/gather_and_multiply/pallas_call | solution.py:527
  65.6 3.9 %round_and_write.1 = (bf16[128,768]{1,0:T(8,128)(2,1)}, bf16[768,6144]{1,0:T(8,128)(2,1)}) custom-call(bf16[128,768]{1,0:T(8,128)(2,1)S(1)} %get-tuple-element.4.gi_ref, f32[6,768,1024]{2,1,0:T(8,128)S(1)} %get-tuple-element.5.dw_ref), custom_call_target="tpu_custom_call" | custom-call | tf_op jit(solution)/shard_map/round_and_write/pallas_call | solution.py:565

commit v6 on v5

--- a/solution.py
+++ b/solution.py
@@ -158,16 +158,16 @@
     def send_x(cb, target, rs):
         remote(xbuf.at[cb], xbuf.at[cb], x_send, rs, target).start()
 
-    x_own.wait()
-    send_x(c, (r, at_col(1, 0)), x_recv.at[0])
-    for dx in (1, 2, 3):
-        send_x(c, (r, at_col(0, dx)), x_recv.at[1])
-
     for i in range(NCH):
         if i:
             grad_pre(i)
         push(0, 0, i, z_up, recv_sem.at[0, i])
         push(0, 0, i, z_dn, recv_sem.at[0, i])
+        if i == 0:
+            x_own.wait()
+            send_x(c, (r, at_col(1, 0)), x_recv.at[0])
+            for dx in (1, 2, 3):
+                send_x(c, (r, at_col(0, dx)), x_recv.at[1])
         push(0, 0, i, y_other, recv_sem.at[2, i])
         share(0, 0, i)
 
@@ -274,12 +274,12 @@
     def to_owner(src, rows, s_sem, cb, j):
         owner_yl, owner_x = cb // NX, lax.rem(cb, NX)
         rel = lax.rem(owner_yl + yl, 2)
-        cp = remote(src, parts.at[j, rel, rows, :], s_sem, own_recv.at[j, rel], (r, owner_yl * NX + owner_x))
+        cp = remote(src, parts.at[j, rel, rows[0], rows[1]], s_sem, own_recv.at[j, rel], (r, owner_yl * NX + owner_x))
         return cp, jnp.logical_or(owner_x != x, owner_yl != yl)
 
     def own_copy(kind):
         cb, row = quarter(kind, x)
-        return to_owner(stage.at[kind], pl.ds(0, tb), own_send.at[kind], cb, row // tb)
+        return to_owner(stage.at[kind], (pl.ds(0, tb), slice(None)), own_send.at[kind], cb, row // tb)
 
     def rs_collect(kind):
         cb, row = quarter(kind, x)
@@ -291,11 +291,17 @@
         cp, away = own_copy(kind)
         pl.when(away)(cp.start)
 
-    def rs2_copy(p, dx):
+    dt = acc.shape[2]
+    pieces = ((0, 0, dt), (1, 0, dt // 2), (1, dt // 2, dt))
+
+    def rs2_copy(m, dx):
+        p, lo, hi = pieces[m]
         cb, row = quarter(FAR, lax.rem(x + dx, NX))
+        cols = pl.ds(lo, hi - lo)
         return remote(
-            sbuf.at[cb, pl.ds(pl.multiple_of(row + p * hb, hb), hb), :], rx.at[FAR, dx - 1, pl.ds(p * hb, hb), :],
-            rs_send, rs2_recv.at[p], (r, at_col(0, dx)),
+            sbuf.at[cb, pl.ds(pl.multiple_of(row + p * hb, hb), hb), cols],
+            rx.at[FAR, dx - 1, pl.ds(p * hb, hb), cols],
+            rs_send, rs2_recv.at[m], (r, at_col(0, dx)),
         )
 
     def rs2_start(p):
@@ -303,23 +309,27 @@
         for q in range(4):
             row = q % 2 * tb + p * hb
             sbuf[2 * plane + q // 2, row:row + hb, :] = acc2[p, q * hb:(q + 1) * hb, :].astype(BF16)
-        for dx in (1, 2, 3):
-            rs2_copy(p, dx).start()
-
-    def own2_copy(p):
+        for m in range(3):
+            if pieces[m][0] == p:
+                for dx in (1, 2, 3):
+                    rs2_copy(m, dx).start()
+
+    def own2_copy(m):
+        p, lo, hi = pieces[m]
         cb, row = quarter(FAR, x)
-        part = pl.ds(p * hb, hb)
-        return to_owner(stage.at[FAR, part, :], part, own_send.at[FAR + p], cb, row // tb)
-
-    def rs2_collect(p):
+        part, cols = pl.ds(p * hb, hb), pl.ds(lo, hi - lo)
+        return to_owner(stage.at[FAR, part, cols], (part, cols), own_send.at[FAR + m], cb, row // tb)
+
+    def rs2_collect(m):
+        p, lo, hi = pieces[m]
         cb, row = quarter(FAR, x)
         row = lax.rem(cb, 2) * tb + row // 2
-        total = acc2[p, pl.ds(pl.multiple_of(row, hb), hb), :]
-        took(rx.at[FAR, :, pl.ds(p * hb, hb), :], rs2_recv.at[p])
+        total = acc2[p, pl.ds(pl.multiple_of(row, hb), hb), lo:hi]
+        took(rx.at[FAR, :, pl.ds(p * hb, hb), pl.ds(lo, hi - lo)], rs2_recv.at[m])
         for dx in (1, 2, 3):
-            total = total + rx[FAR, dx - 1, p * hb:(p + 1) * hb, :].astype(F32)
-        stage[FAR, p * hb:(p + 1) * hb, :] = total.astype(BF16)
-        cp, away = own2_copy(p)
+            total = total + rx[FAR, dx - 1, p * hb:(p + 1) * hb, lo:hi].astype(F32)
+        stage[FAR, p * hb:(p + 1) * hb, lo:hi] = total.astype(BF16)
+        cp, away = own2_copy(m)
         pl.when(away)(cp.start)
 
     def rs_finish():
@@ -440,6 +450,9 @@
             rs_collect(CROSS)
         if n == 19:
             rs2_collect(0)
+        if n == 20:
+            rs2_collect(1)
+            rs2_collect(2)
 
     def between(n):
         if n == 3:
@@ -480,7 +493,6 @@
         choose(step, between, 0, STEPS)
         pl.when(busy(MM2, step))(lambda: mm2(step))
 
-    rs2_collect(1)
     rs_finish()
 
     assert n_sent[0] == N_SENDS and n_sent2[0] == N_SENDS2
@@ -492,7 +504,7 @@
         (rs_send, rx),
     ):
         remote(ref, ref, sem, recv_sem.at[0, 0], core_other).wait_send()
-    last = [own_copy(kind) for kind in (OWN, NEAR, CROSS)] + [own2_copy(p) for p in range(2)]
+    last = [own_copy(kind) for kind in (OWN, NEAR, CROSS)] + [own2_copy(m) for m in range(3)]
     for cp, away in last:
         pl.when(away)(cp.wait_send)
 
@@ -503,17 +515,15 @@
 
 
 def out_kernel(gi_ref, dw_ref, gi_out, dw_out, buf, sem):
-    cw = dw_ref.shape[2]
-    gi_copy = pltpu.make_async_copy(gi_ref, gi_out, sem.at[NCH])
+    rows, cw = dw_ref.shape[1] // 2, dw_ref.shape[2]
+    gi_copy = pltpu.make_async_copy(gi_ref, gi_out, sem.at[0])
     gi_copy.start()
-    copies = []
     for i in range(NCH):
-        buf[i] = dw_ref[i].astype(buf.dtype)
-        cp = pltpu.make_async_copy(buf.at[i], dw_out.at[:, pl.ds(i * cw, cw)], sem.at[i])
-        cp.start()
-        copies.append(cp)
-    for cp in copies:
-        cp.wait()
+        for h in range(2):
+            part = pl.ds(h * rows, rows)
+            buf[i, h * rows:(h + 1) * rows] = dw_ref[i, h * rows:(h + 1) * rows].astype(buf.dtype)
+            pltpu.make_async_copy(buf.at[i, part], dw_out.at[part, pl.ds(i * cw, cw)], sem.at[1]).start()
+    pltpu.make_async_copy(buf, buf, sem.at[1]).wait()
     gi_copy.wait()
 
 
@@ -553,8 +563,8 @@
             dma((2,)),
             dma,
             dma((3,)),
-            dma((2,)),
-            dma((5,)),
+            dma((3,)),
+            dma((6,)),
             dma((2, 2)),
         ],
         compiler_params=pltpu.CompilerParams(
@@ -570,7 +580,7 @@
         ),
         in_specs=[vmem, vmem],
         out_specs=(hbm, hbm),
-        scratch_shapes=[pltpu.VMEM((NCH, dt, cw), BF16), dma((NCH + 1,))],
+        scratch_shapes=[pltpu.VMEM((NCH, dt, cw), BF16), dma((2,))],
         compiler_params=pltpu.CompilerParams(vmem_limit_bytes=20 * 2**20),
         name="round_and_write",
     )(gi, dw)

time: 69.6 us -> 69.2 us (level)
  no operation moved by 1% of the time
where the time goes in v6:
time: 69.2 us; the launch traced here: 69.1 us
  Pallas kernels  68.5 us (99%)
    pallas_call x1, Pallas kernels, body(): pl.pallas_call(main_kernel, out_shape=(pltpu.VMEM((ob, dt), BF16), pltpu....  64.7 us
    pallas_call x1, Pallas kernels, body(): pl.pallas_call(out_kernel, out_shape=(jax.ShapeDtypeStruct((ob, dt), BF16...  3.71 us

profile of v6, /device:TPU:8, one launch (start us, length us, event | category | flops | bytes accessed | tf_op | source)
XLA Modules:
  0.0 69.1 jit_solution(15935032405269099418)
XLA Ops:
  0.6 64.7 %gather_and_multiply.1 = (bf16[128,768]{1,0:T(8,128)(2,1)S(1)}, f32[6,768,1024]{2,1,0:T(8,128)S(1)}) custom-call(bf16[64,6144]{1,0:T(8,128)(2,1)} %g_hbm.1, bf16[64,6144]{1,0:T(8,128)(2,1)} %v_hbm.1, bf16[128,768]{1,0:T(8,128)(2,1)} %x_hbm.1, bf16[768,6144]{1,0:T(8,128)(2,1)} %w_hbm.1), custom_call_target="tpu_custom_call" | custom-call | tf_op jit(solution)/shard_map/gather_and_multiply/pallas_call | solution.py:537
  65.4 3.7 %round_and_write.1 = (bf16[128,768]{1,0:T(8,128)(2,1)}, bf16[768,6144]{1,0:T(8,128)(2,1)}) custom-call(bf16[128,768]{1,0:T(8,128)(2,1)S(1)} %get-tuple-element.4.gi_ref, f32[6,768,1024]{2,1,0:T(8,128)S(1)} %get-tuple-element.5.dw_ref), custom_call_target="tpu_custom_call" | custom-call | tf_op jit(solution)/shard_map/round_and_write/pallas_call | solution.py:575

commit v7 on v6

--- a/solution.py
+++ b/solution.py
@@ -25,13 +25,13 @@
     ((OWN, 2), None, (OWN, 2)),
     (None, None, (CROSS, 0)),
     ((CROSS, 1), None, (CROSS, 1)),
-    ((CROSS, 2), None, (CROSS, 2)),
+    ((CROSS, 2), None, None),
     (None, (0, 0), None),
     (None, (0, 1), None),
     (None, (0, 2), None),
     (None, (1, 2), None),
     (None, (1, 0), None),
-    (None, (1, 1), None),
+    (None, (1, 1), (CROSS, 2)),
     (None, None, (FAR, 2)),
     (None, None, (FAR, 0)),
     (None, None, (FAR, 1)),
@@ -448,7 +448,7 @@
             rs_collect(OWN)
         if n == 15:
             rs_collect(CROSS)
-        if n == 19:
+        if n == 18:
             rs2_collect(0)
         if n == 20:
             rs2_collect(1)

time: 69.2 us -> 69.2 us (level)
  no operation moved by 1% of the time
where the time goes in v7:
time: 69.2 us; the launch traced here: 69.1 us
  Pallas kernels  68.5 us (99%)
    pallas_call x1, Pallas kernels, body(): pl.pallas_call(main_kernel, out_shape=(pltpu.VMEM((ob, dt), BF16), pltpu....  64.7 us
    pallas_call x1, Pallas kernels, body(): pl.pallas_call(out_kernel, out_shape=(jax.ShapeDtypeStruct((ob, dt), BF16...  3.71 us

profile of v7, /device:TPU:8, one launch (start us, length us, event | category | flops | bytes accessed | tf_op | source)
XLA Modules:
  0.0 69.1 jit_solution(10026943511832201949)
XLA Ops:
  0.6 64.7 %gather_and_multiply.1 = (bf16[128,768]{1,0:T(8,128)(2,1)S(1)}, f32[6,768,1024]{2,1,0:T(8,128)S(1)}) custom-call(bf16[64,6144]{1,0:T(8,128)(2,1)} %g_hbm.1, bf16[64,6144]{1,0:T(8,128)(2,1)} %v_hbm.1, bf16[128,768]{1,0:T(8,128)(2,1)} %x_hbm.1, bf16[768,6144]{1,0:T(8,128)(2,1)} %w_hbm.1), custom_call_target="tpu_custom_call" | custom-call | tf_op jit(solution)/shard_map/gather_and_multiply/pallas_call | solution.py:537
  65.4 3.7 %round_and_write.1 = (bf16[128,768]{1,0:T(8,128)(2,1)}, bf16[768,6144]{1,0:T(8,128)(2,1)}) custom-call(bf16[128,768]{1,0:T(8,128)(2,1)S(1)} %get-tuple-element.4.gi_ref, f32[6,768,1024]{2,1,0:T(8,128)S(1)} %get-tuple-element.5.dw_ref), custom_call_target="tpu_custom_call" | custom-call | tf_op jit(solution)/shard_map/round_and_write/pallas_call | solution.py:575
